TPU v7x, 32 devices: a whole 2x2x4 slice. The times are simulated.
32 devices in a mesh: lat: 8 (over z, y), lon: 4 (over x, core).
Axes of the slice: x: 2, y: 2, z: 4, core: 2. Of those that a mesh axis runs over, the one named last changes fastest.
Arguments:
- thickness: float32 [2, 704, 5760], P(None, 'lat', 'lon'), may hold values from 0.5 to 1.5
- zonal_wind: float32 [2, 704, 5760], P(None, 'lat', 'lon'), may hold values from -3 to 3
- merid_wind: float32 [2, 704, 5760], P(None, 'lat', 'lon'), may hold values from -3 to 3
- tracers: float32 [8, 2, 704, 5760], P(None, None, 'lat', 'lon'), may hold values from 0.1 to 2
- cutoffs: int32 [176], replicated, may hold values from 64 to 512
Outputs:
- new_thickness: float32 [2, 704, 5760], P(None, 'lat', 'lon')
- new_zonal: float32 [2, 704, 5760], P(None, 'lat', 'lon')
- new_merid: float32 [2, 704, 5760], P(None, 'lat', 'lon')
- tracer_mass: float32 [8, 2, 704, 5760], P(None, None, 'lat', 'lon')
All inputs are finite; a program needn't handle non-finite values.
Results may differ from a plain program's by a relative error of at most 0.0003.
Values sent between devices are 32-bit elements; how exact they have to be, the bound alone decides.
A program may use at most 192 MiB of HBM per device.

v0:
```python
import math

import jax
import jax.numpy as jnp
from jax import lax
from jax.sharding import PartitionSpec as P

NLON = 5760
KMAX = 512
SUBSTEPS = 3


LAT_EDGE = 85.0 * math.pi / 180.0
PRESSURE_PUSH = 0.08
DIVERGE_RATE = 0.08
COURANT_RATE = 0.3


def padded_2(cells, sides, width):
    for axis, dim in sides:
        count = lax.axis_size(axis)
        head = lax.slice_in_dim(cells, 0, width, axis=dim)
        tail = lax.slice_in_dim(cells, cells.shape[dim] - width, cells.shape[dim], axis=dim)
        cells = jnp.concatenate(
            [
                lax.ppermute(tail, axis, [(i, (i + 1) % count) for i in range(count)]),
                cells,
                lax.ppermute(head, axis, [((i + 1) % count, i) for i in range(count)]),
            ],
            axis=dim,
        )
    return cells


def passed_along(value, axis, steps):
    count = lax.axis_size(axis)
    pairs = [(source, (source + steps) % count) for source in range(count)]
    return lax.ppermute(value, axis, pairs)


def from_behind(array, axis, by):
    length = lax.axis_size(axis)
    pairs = [(i, i + by) for i in range(length) if 0 <= i + by < length]
    return lax.ppermute(array, axis, pairs)


def center_cos(global_rows, total_rows):
    return jnp.cos(((2 * global_rows + 1).astype(jnp.float32) / total_rows - 1.0) * LAT_EDGE)


def face_cos(global_rows, total_rows):
    return jnp.cos(((2 * global_rows + 2).astype(jnp.float32) / total_rows - 1.0) * LAT_EDGE)


def fourier_basis(columns, length, modes):
    waves = jnp.arange(modes, dtype=jnp.int32)
    phase = columns[:, None] * waves[None, :] % length
    angle = phase.astype(jnp.float32) * (2.0 * math.pi / length)
    return jnp.concatenate([jnp.cos(angle), jnp.sin(angle)], axis=1)


def spectral_weights(row_cut, length, modes):
    waves = jnp.arange(modes, dtype=jnp.int32)
    scaled = jnp.where(waves == 0, 1.0, 2.0).astype(jnp.float32) / length
    keep_mode = waves[None, :] < row_cut[:, None]
    weights = jnp.where(keep_mode, scaled[None, :], jnp.zeros_like(scaled)[None, :])
    return jnp.concatenate([weights, weights], axis=1)


def ppm_faces(values, courant, along_dim, length):

    def part(offset):
        return lax.slice_in_dim(values, 2 + offset, 3 + offset + length, axis=along_dim)

    back_two, back_one, center, ahead_one, ahead_two, ahead_three = [
        part(offset) for offset in range(-2, 4)
    ]
    left_edge = 7.0 / 12.0 * (back_one + center) - 1.0 / 12.0 * (back_two + ahead_one)
    middle_edge = 7.0 / 12.0 * (center + ahead_one) - 1.0 / 12.0 * (back_one + ahead_two)
    right_edge = 7.0 / 12.0 * (ahead_one + ahead_two) - 1.0 / 12.0 * (center + ahead_three)
    slope_here = middle_edge - left_edge
    curve_here = 6.0 * center - 3.0 * (left_edge + middle_edge)
    slope_next = right_edge - middle_edge
    curve_next = 6.0 * ahead_one - 3.0 * (middle_edge + right_edge)
    clipped = jnp.clip(courant, -1.0, 1.0)
    upwind = middle_edge - 0.5 * clipped * (slope_here - (1.0 - clipped * (2.0 / 3.0)) * curve_here)
    downwind = middle_edge - 0.5 * clipped * (
        slope_next + (1.0 + clipped * (2.0 / 3.0)) * curve_next
    )
    return jnp.where(clipped > 0.0, upwind, downwind)


def outside_zero(extended, margin, total_rows, rows_dev):
    first_row = lax.axis_index("lat") * rows_dev - margin
    ext_rows = first_row + jnp.arange(rows_dev + 2 * margin, dtype=jnp.int32)
    inside = (ext_rows >= 0) & (ext_rows < total_rows)
    return jnp.where(inside[:, None], extended, jnp.zeros_like(extended))


def spectral_filter(block, global_rows, cutoffs, total_rows):
    fields, levels, count, width = block.shape
    polar = total_rows // 8
    slot_of_row = jnp.where(global_rows < polar, global_rows, global_rows - total_rows + 2 * polar)
    slot_index = jnp.arange(2 * polar, dtype=jnp.int32)
    matches = slot_of_row[:, None] == slot_index[None, :]
    row_cut = jnp.sum(
        jnp.where(matches, cutoffs[None, :], jnp.zeros_like(cutoffs)[None, :]), axis=1
    )
    is_polar = (global_rows < polar) | (global_rows >= total_rows - polar)
    flat = block.reshape(fields * levels * count, width)
    flat_cut = jnp.broadcast_to(row_cut, (fields, levels, count)).reshape(-1)
    columns = lax.axis_index("lon") * width + jnp.arange(width, dtype=jnp.int32)
    basis = fourier_basis(columns, NLON, KMAX)
    partial_sums = jnp.dot(
        flat, basis, precision=lax.Precision.HIGHEST, preferred_element_type=jnp.float32
    )
    coeffs = lax.psum(partial_sums, "lon") * spectral_weights(flat_cut, NLON, KMAX)
    smooth_flat = jnp.dot(
        coeffs, basis.T, precision=lax.Precision.HIGHEST, preferred_element_type=jnp.float32
    )
    smooth = smooth_flat.reshape(block.shape)
    return jnp.where(is_polar[:, None], smooth, block)


def local(thickness, zonal_wind, merid_wind, tracers, cutoffs):
    levels, rows_dev, width = thickness.shape
    total_rows = rows_dev * lax.axis_size("lat")
    first_row = lax.axis_index("lat") * rows_dev
    own_rows = first_row + jnp.arange(rows_dev, dtype=jnp.int32)
    cos_center = center_cos(own_rows, total_rows)[:, None]
    wall_center = (own_rows < total_rows - 1).astype(jnp.float32)[:, None]
    face_rows = first_row - 1 + jnp.arange(rows_dev + 1, dtype=jnp.int32)
    cos_face = face_cos(face_rows, total_rows)[:, None]
    wall_face = ((face_rows >= 0) & (face_rows < total_rows - 1)).astype(jnp.float32)[:, None]
    pressure = thickness
    zonal = zonal_wind
    merid = merid_wind
    mass_x = jnp.zeros((levels, rows_dev, width + 1), jnp.float32)
    mass_y = jnp.zeros((levels, rows_dev + 1, width), jnp.float32)
    wind_x = jnp.zeros((levels, rows_dev, width + 1), jnp.float32)
    wind_y = jnp.zeros((levels, rows_dev + 1, width), jnp.float32)
    for substep in range(SUBSTEPS):
        padded = padded_2(pressure, (("lat", 1), ("lon", 2)), 1)
        padded = outside_zero(padded, 1, total_rows, rows_dev)
        here = padded[:, 1:-1, 1:-1]
        zonal = zonal - PRESSURE_PUSH / cos_center * (padded[:, 1:-1, 2:] - here)
        merid = (merid - PRESSURE_PUSH * (padded[:, 2:, 1:-1] - here)) * wall_center
        stacked = jnp.stack([zonal, merid])
        stacked = spectral_filter(stacked, own_rows, cutoffs, total_rows)
        zonal = stacked[0]
        merid = stacked[1]
        west_column = passed_along(zonal[:, :, width - 1 :], "lon", 1)
        south_row = from_behind(merid[:, rows_dev - 1 :, :], "lat", 1)
        east_wind = jnp.concatenate([west_column, zonal], axis=2)
        north_wind = jnp.concatenate([south_row, merid], axis=1)
        flux_x = 0.5 * (padded[:, 1:-1, :-1] + padded[:, 1:-1, 1:]) * east_wind
        flux_y = (
            0.5 * (padded[:, :-1, 1:-1] + padded[:, 1:, 1:-1]) * north_wind * cos_face * wall_face
        )
        pressure = (
            pressure
            - DIVERGE_RATE / cos_center * (flux_x[:, :, 1:] - flux_x[:, :, :-1])
            - DIVERGE_RATE / cos_center * (flux_y[:, 1:, :] - flux_y[:, :-1, :])
        )
        mass_x = mass_x + flux_x
        mass_y = mass_y + flux_y
        wind_x = wind_x + east_wind
        wind_y = wind_y + north_wind
    courant_x = COURANT_RATE / cos_center * wind_x
    courant_y = COURANT_RATE * wind_y
    extended = padded_2(tracers, (("lat", 2), ("lon", 3)), 3)
    extended = outside_zero(extended, 3, total_rows, rows_dev)
    faces_x = ppm_faces(extended[:, :, 3:-3, :], courant_x, 3, width)
    faces_y = ppm_faces(extended[:, :, :, 3:-3], courant_y, 2, rows_dev)
    carried_x = mass_x * faces_x
    carried_y = mass_y * faces_y
    tracer_mass = (
        tracers * thickness
        - DIVERGE_RATE / cos_center * (carried_x[..., 1:] - carried_x[..., :-1])
        - DIVERGE_RATE / cos_center * (carried_y[..., 1:, :] - carried_y[..., :-1, :])
    )
    return (pressure, zonal, merid, tracer_mass)


def solution(mesh):
    return jax.shard_map(
        local,
        mesh=mesh,
        in_specs=(
            P(None, "lat", "lon"),
            P(None, "lat", "lon"),
            P(None, "lat", "lon"),
            P(None, None, "lat", "lon"),
            P(),
        ),
        out_specs=(
            P(None, "lat", "lon"),
            P(None, "lat", "lon"),
            P(None, "lat", "lon"),
            P(None, None, "lat", "lon"),
        ),
        check_vma=False,
    )
```

profile of v0, /device:TPU:0, one launch (start us, length us, event | category | flops | bytes accessed | tf_op | source)
XLA Modules:
  0.0 451.9 jit_solution(13285749847733462753)
XLA Ops:
  8.2 6.1 %collective-permute-start.1 = (f32[2,1,1440]{2,1,0:T(1,128)S(1)}, f32[2,1,1440]{2,1,0:T(1,128)S(1)}, u32[]{:S(2)}, u32[]{:S(2)}) collective-permute-start(f32[2,1,1440]{2,1,0:T(1,128)S(1)} %get-tuple-element.53), channel_id=1, source_target_pairs={{4,0},{8,4},{12,8},{16,12},{20,16},{24,20},{28,24},{0,28},{5,1},{9... | collective-permute-start | bytes 34568 | tf_op jit(solution)/shard_map/ppermute | solution.py:28
  14.3 13.8 %fusion.17 = (f32[1440,512]{1,0:T(8,128)S(1)}, f32[1440,512]{1,0:T(8,128)}) fusion(s32[1440]{0:T(1024)S(1)} %iota_add_fusion), kind=kLoop, calls=%fused_computation.29 | loop fusion | flops 6635520 | bytes 5904000 | tf_op jit(solution)/shard_map/cos | solution.py:59
  30.7 1.7 collective-permute-start.3
  32.4 2.3 collective-permute-done.2
  34.8 2.4 concatenate.113
  42.7 8.3 %fusion.82 = f32[352,1024]{1,0:T(8,128)} fusion(f32[352,1440]{1,0:T(8,128)S(1)} %bitcast.46, f32[1440,512]{1,0:T(8,128)S(1)} %copy-done, f32[1440,512]{1,0:T(8,128)S(1)} %get-tuple-element.54), kind=kOutput, calls=%fused_computation.140 | convolution fusion | flops 6230016000 | bytes 9367552 | tf_op jit(solution)/shard_map/dot_general | solution.py:114
  53.0 40.8 %all-reduce.4.cloned.1.call-done = f32[352,1024]{1,0:T(8,128)} async-done(((f32[352,1024]{1,0:T(8,128)}), f32[352,1024]{1,0:T(8,128)}) %all-reduce.4.cloned.1.call-update) | async-done | bytes 1441808 | tf_op jit(solution)/shard_map/psum | solution.py:117
  93.8 10.0 %fusion.22 = f32[352,1440]{1,0:T(8,128)S(1)} fusion(f32[352,1024]{1,0:T(8,128)} %all-reduce.4.cloned.1.call-done, f32[352,512]{1,0:T(8,128)} %fusion.79, f32[1440,512]{1,0:T(8,128)} %get-tuple-element.55, f32[1440,512]{1,0:T(8,128)S(1)} %get-tuple-element.54), kind=kOutput, calls=%fused_computation.38 | convolution fusion | flops 6230736896 | bytes 10088448 | tf_op jit(solution)/shard_map/dot_general | solution.py:118
  105.8 3.4 collective-permute-start.5
  113.1 4.5 collective-permute-start.7
  118.9 5.0 %collective-permute-done.6 = f32[2,1,1440]{2,1,0:T(1,128)S(1)} collective-permute-done((f32[2,1,1440]{2,1,0:T(1,128)S(1)}, f32[2,1,1440]{2,1,0:T(1,128)S(1)}, u32[]{:S(2)}, u32[]{:S(2)}) %collective-permute-start.6) | collective-permute-done | bytes 11552 | tf_op jit(solution)/shard_map/ppermute | solution.py:26
  125.1 2.1 collective-permute-start.9
  127.2 1.9 collective-permute-done.8
  129.4 2.4 concatenate.119
  137.4 8.3 %fusion.81 = f32[352,1024]{1,0:T(8,128)} fusion(f32[352,1440]{1,0:T(8,128)S(1)} %bitcast.47, f32[1440,512]{1,0:T(8,128)S(1)} %copy-done.1, f32[1440,512]{1,0:T(8,128)S(1)} %get-tuple-element.54), kind=kOutput, calls=%fused_computation.139 | convolution fusion | flops 6230016000 | bytes 9367552 | tf_op jit(solution)/shard_map/dot_general | solution.py:114
  146.0 38.3 %all-reduce.6.cloned.1.call-done = f32[352,1024]{1,0:T(8,128)} async-done(((f32[352,1024]{1,0:T(8,128)}), f32[352,1024]{1,0:T(8,128)}) %all-reduce.6.cloned.1.call-update) | async-done | bytes 1441808 | tf_op jit(solution)/shard_map/psum | solution.py:117
  184.3 10.0 %fusion.24 = f32[352,1440]{1,0:T(8,128)S(1)} fusion(f32[352,1024]{1,0:T(8,128)} %all-reduce.6.cloned.1.call-done, f32[352,512]{1,0:T(8,128)} %fusion.79, f32[1440,512]{1,0:T(8,128)} %get-tuple-element.55, f32[1440,512]{1,0:T(8,128)S(1)} %get-tuple-element.54), kind=kOutput, calls=%fused_computation.39 | convolution fusion | flops 6230736896 | bytes 10088448 | tf_op jit(solution)/shard_map/dot_general | solution.py:118
  196.2 3.4 collective-permute-start.11
  203.5 4.4 collective-permute-start.13
  209.3 5.0 %collective-permute-done.12 = f32[2,1,1440]{2,1,0:T(1,128)S(1)} collective-permute-done((f32[2,1,1440]{2,1,0:T(1,128)S(1)}, f32[2,1,1440]{2,1,0:T(1,128)S(1)}, u32[]{:S(2)}, u32[]{:S(2)}) %collective-permute-start.12) | collective-permute-done | bytes 11552 | tf_op jit(solution)/shard_map/ppermute | solution.py:26
  215.5 1.9 collective-permute-start.15
  217.4 2.1 collective-permute-done.14
  219.6 2.4 concatenate.123
  227.6 8.3 %fusion.80 = f32[352,1024]{1,0:T(8,128)} fusion(f32[352,1440]{1,0:T(8,128)S(1)} %bitcast.48, f32[1440,512]{1,0:T(8,128)S(1)} %copy-done.2, f32[1440,512]{1,0:T(8,128)S(1)} %get-tuple-element.54), kind=kOutput, calls=%fused_computation.138 | convolution fusion | flops 6230016000 | bytes 9367552 | tf_op jit(solution)/shard_map/dot_general | solution.py:114
  239.2 2.0 collective-permute-start.18
  241.2 11.3 %copy.28 = f32[8,2,88,1440]{2,0,3,1:T(8,128)} copy(f32[8,2,88,1440]{3,2,1,0:T(8,128)} %param.8) | data formatting | bytes 16220160 | tf_op args[3]
  252.6 2.8 copy.27
  255.5 6.6 %copy.35 = f32[8,2,3,1440]{2,0,3,1:T(8,128)} copy(f32[8,2,3,1440]{3,0,2,1:T(8,128)S(1)} %collective-permute-done.19) | data formatting | bytes 552960 | tf_op jit(solution)/shard_map/ppermute | solution.py:28
  262.0 7.5 %copy.33 = f32[8,2,3,1440]{2,0,3,1:T(8,128)} copy(f32[8,2,3,1440]{3,0,2,1:T(8,128)} %collective-permute-done.18) | data formatting | bytes 552960 | tf_op jit(solution)/shard_map/ppermute | solution.py:26
  272.3 2.3 all-reduce.8.cloned.1.call-done
  274.6 10.0 %fusion.26 = f32[352,1440]{1,0:T(8,128)S(1)} fusion(f32[352,1024]{1,0:T(8,128)} %all-reduce.8.cloned.1.call-done, f32[352,512]{1,0:T(8,128)} %fusion.79, f32[1440,512]{1,0:T(8,128)} %get-tuple-element.55, f32[1440,512]{1,0:T(8,128)S(1)} %get-tuple-element.54), kind=kOutput, calls=%fused_computation.40 | convolution fusion | flops 6230736896 | bytes 10088448 | tf_op jit(solution)/shard_map/dot_general | solution.py:118
  285.4 2.0 slice-done.2
  287.4 16.2 %maximum_select_fusion = f32[8,2,94,1446]{2,0,3,1:T(8,128)} fusion(f32[8,2,94,3]{2,0,3,1:T(8,128)S(1)} %collective-permute-done.21, f32[8,2,3,1440]{2,0,3,1:T(8,128)} %copy.35, f32[8,2,88,1440]{2,0,3,1:T(8,128)S(1)} %bitcast.42, f32[8,2,3,1440]{2,0,3,1:T(8,128)} %copy.33, f32[8,2,94,3]{2,0,3,1:T(8,128)S(1)} %collective-permute-done.20, ...), kind=kLoop, calls=%fused_computation | loop fusion | flops 10873920 | bytes 17398366 | tf_op jit(solution)/shard_map/jit(_where)/select_n | solution.py:97
  303.6 3.8 collective-permute-start.17
  311.2 1.6 copy.37
  312.9 2.9 copy.36
  315.8 3.5 add_add_fusion.1
  319.4 2.8 copy.29
  322.8 33.9 %select_multiply_fusion = f32[8,2,88,1441]{2,0,3,1:T(8,128)} fusion(f32[8,2,94,1446]{2,0,3,1:T(8,128)} %maximum_select_fusion, f32[2,88,1441]{1,2,0:T(8,128)} %copy.38, f32[2,88,1441]{1,2,0:T(8,128)} %copy.37, f32[2,88,1441]{1,2,0:T(8,128)} %copy.36, f32[2,88,1441]{1,2,0:T(8,128)} %copy.29, pred[2,88,1441]{1,2,0:T(8,128)(4,1)S(1)} %copy.30), kind=kLoop, calls=%fused_computation.7 | loop fusion | flops 71012480 | bytes 61121456 | tf_op jit(solution)/shard_map/mul | solution.py:175
  358.0 1.8 broadcast_multiply_fusion
  359.9 2.9 copy.43
  364.3 2.9 copy.41
  367.3 3.7 add_add_fusion
  371.0 3.1 copy.39
  374.7 31.9 %select_multiply_fusion.1 = f32[8,2,89,1440]{2,0,3,1:T(8,128)} fusion(f32[8,2,94,1446]{2,0,3,1:T(8,128)} %maximum_select_fusion, f32[2,89,1440]{1,2,0:T(8,128)S(1)} %copy-done.49, f32[2,89,1440]{1,2,0:T(8,128)} %copy.42, f32[2,89,1440]{1,2,0:T(8,128)} %copy.41, f32[2,89,1440]{1,2,0:T(8,128)} %copy.39, pred[2,89,1440]{1,2,0:T(8,128)(4,1)S(1)} %copy.40), kind=kLoop, calls=%fused_computation.20 | loop fusion | flops 71769600 | bytes 61773120 | tf_op jit(solution)/shard_map/mul | solution.py:176
  406.6 23.9 %fusion.5 = f32[8,2,88,1440]{2,0,3,1:T(8,128)} fusion(f32[8,2,89,1440]{2,0,3,1:T(8,128)} %select_multiply_fusion.1, f32[8,2,88,1441]{2,0,3,1:T(8,128)} %select_multiply_fusion, f32[8,2,88,1440]{2,0,3,1:T(8,128)} %copy.28, f32[88]{0:T(128)S(1)} %fusion.83, f32[2,88,1440]{1,2,0:T(8,128)S(1)} %copy-done.48), kind=kLoop, calls=%fused_computation.10 | loop fusion | flops 14192640 | bytes 49674592 | tf_op jit(solution)/shard_map/sub | solution.py:178
  430.6 11.5 %copy.44 = f32[8,2,88,1440]{3,2,1,0:T(8,128)} copy(f32[8,2,88,1440]{2,0,3,1:T(8,128)} %fusion.5) | data formatting | bytes 16220160
  442.1 3.2 fusion.41
  (217 shorter events, 54.4 us)
Async XLA Ops:
  7.2 86.7 %all-reduce.4.cloned.1.call-start = ((), (), s32[]{:S(2)}) async-start(), calls=%async_computation | async-start | bytes 2883584 | tf_op jit(solution)/shard_map/psum | solution.py:117
  8.2 19.9 %collective-permute-start.1 = (f32[2,1,1440]{2,1,0:T(1,128)S(1)}, f32[2,1,1440]{2,1,0:T(1,128)S(1)}, u32[]{:S(2)}, u32[]{:S(2)}) collective-permute-start(f32[2,1,1440]{2,1,0:T(1,128)S(1)} %get-tuple-element.53), channel_id=1, source_target_pairs={{4,0},{8,4},{12,8},{16,12},{20,16},{24,20},{28,24},{0,28},{5,1},{9... | collective-permute-start | bytes 34568 | tf_op jit(solution)/shard_map/ppermute | solution.py:28
  14.2 13.9 %collective-permute-start = (f32[2,1,1440]{2,1,0:T(1,128)S(1)}, f32[2,1,1440]{2,1,0:T(1,128)S(1)}, u32[]{:S(2)}, u32[]{:S(2)}) collective-permute-start(f32[2,1,1440]{2,1,0:T(1,128)S(1)} %get-tuple-element.52), channel_id=1, source_target_pairs={{0,4},{4,8},{8,12},{12,16},{16,20},{20,24},{24,28},{28,0},{1,5},{5... | collective-permute-start | bytes 34568 | tf_op jit(solution)/shard_map/ppermute | solution.py:26
  30.6 4.1 collective-permute-start.2
  30.7 4.1 collective-permute-start.3
  51.0 133.2 %all-reduce.6.cloned.1.call-start = ((), (), s32[]{:S(2)}) async-start(), calls=%async_computation.1 | async-start | bytes 2883584 | tf_op jit(solution)/shard_map/psum | solution.py:117
  93.8 10.0 %copy-start.41 = (f32[1,2,88,1440]{3,2,1,0:T(8,128)S(1)}, f32[1,2,88,1440]{3,2,1,0:T(8,128)}, u32[]{:S(2)}) copy-start(f32[1,2,88,1440]{3,2,1,0:T(8,128)} %copy-done.40) | copy-start | bytes 3041284
  93.8 10.0 %copy-start.43 = (f32[1,2,88,1440]{3,2,1,0:T(8,128)S(1)}, f32[1,2,88,1440]{3,2,1,0:T(8,128)}, u32[]{:S(2)}) copy-start(f32[1,2,88,1440]{3,2,1,0:T(8,128)} %copy-done.42) | copy-start | bytes 3041284
  104.3 5.4 %copy-start.6 = (f32[2,90,1442]{2,1,0:T(8,128)S(1)}, f32[2,90,1442]{2,1,0:T(8,128)}, u32[]{:S(2)}) copy-start(f32[2,90,1442]{2,1,0:T(8,128)} %copy-done.5) | copy-start | bytes 3114724
  105.6 5.0 %copy-start.31 = (f32[2,88,1440]{2,1,0:T(8,128)}, f32[2,88,1440]{2,1,0:T(8,128)S(1)}, u32[]{:S(2)}) copy-start(f32[2,88,1440]{2,1,0:T(8,128)S(1)} %get-tuple-element.33) | copy-start | bytes 3041284
  105.7 4.0 collective-permute-start.4
  105.8 4.8 %collective-permute-start.5 = (f32[2,1,1440]{2,1,0:T(1,128)S(1)}, f32[2,1,1440]{2,1,0:T(1,128)S(1)}, u32[]{:S(2)}, u32[]{:S(2)}) collective-permute-start(f32[2,1,1440]{2,1,0:T(1,128)S(1)} %slice.336), channel_id=1, source_target_pairs={{0,4},{4,8},{8,12},{12,16},{16,20},{20,24},{24,28},{1,5},{5,9},{9,... | collective-permute-start | bytes 34568 | tf_op jit(solution)/shard_map/ppermute | solution.py:44
  113.0 11.1 %copy-start.26 = (f32[2,88,1440]{2,1,0:T(8,128)}, f32[2,88,1440]{2,1,0:T(8,128)S(1)}, u32[]{:S(2)}) copy-start(f32[2,88,1440]{2,1,0:T(8,128)S(1)} %fusion.67) | copy-start | bytes 3041284
  113.1 5.9 %collective-permute-start.7 = (f32[2,1,1440]{2,1,0:T(1,128)S(1)}, f32[2,1,1440]{2,1,0:T(1,128)S(1)}, u32[]{:S(2)}, u32[]{:S(2)}) collective-permute-start(f32[2,1,1440]{2,1,0:T(1,128)S(1)} %get-tuple-element.51), channel_id=1, source_target_pairs={{4,0},{8,4},{12,8},{16,12},{20,16},{24,20},{28,24},{0,28},{5,1},{9... | collective-permute-start | bytes 34568 | tf_op jit(solution)/shard_map/ppermute | solution.py:28
  117.5 6.4 %collective-permute-start.6 = (f32[2,1,1440]{2,1,0:T(1,128)S(1)}, f32[2,1,1440]{2,1,0:T(1,128)S(1)}, u32[]{:S(2)}, u32[]{:S(2)}) collective-permute-start(f32[2,1,1440]{2,1,0:T(1,128)S(1)} %get-tuple-element.50), channel_id=1, source_target_pairs={{0,4},{4,8},{8,12},{12,16},{16,20},{20,24},{24,28},{28,0},{1,5},{5... | collective-permute-start | bytes 34568 | tf_op jit(solution)/shard_map/ppermute | solution.py:26
  125.1 4.0 collective-permute-start.8
  125.1 4.3 collective-permute-start.9
  145.7 128.9 %all-reduce.8.cloned.1.call-start = ((), (), s32[]{:S(2)}) async-start(), calls=%async_computation.2 | async-start | bytes 2883584 | tf_op jit(solution)/shard_map/psum | solution.py:117
  184.3 10.0 %copy-start.45 = (f32[1,2,88,1440]{3,2,1,0:T(8,128)S(1)}, f32[1,2,88,1440]{3,2,1,0:T(8,128)}, u32[]{:S(2)}) copy-start(f32[1,2,88,1440]{3,2,1,0:T(8,128)} %copy-done.44) | copy-start | bytes 3041284
  184.3 10.0 %copy-start.47 = (f32[1,2,88,1440]{3,2,1,0:T(8,128)S(1)}, f32[1,2,88,1440]{3,2,1,0:T(8,128)}, u32[]{:S(2)}) copy-start(f32[1,2,88,1440]{3,2,1,0:T(8,128)} %copy-done.46) | copy-start | bytes 3041284
  194.7 5.4 %copy-start.8 = (f32[2,90,1442]{2,1,0:T(8,128)S(1)}, f32[2,90,1442]{2,1,0:T(8,128)}, u32[]{:S(2)}) copy-start(f32[2,90,1442]{2,1,0:T(8,128)} %copy-done.7) | copy-start | bytes 3114724
  196.1 4.0 collective-permute-start.10
  196.2 4.8 %collective-permute-start.11 = (f32[2,1,1440]{2,1,0:T(1,128)S(1)}, f32[2,1,1440]{2,1,0:T(1,128)S(1)}, u32[]{:S(2)}, u32[]{:S(2)}) collective-permute-start(f32[2,1,1440]{2,1,0:T(1,128)S(1)} %slice.355), channel_id=1, source_target_pairs={{0,4},{4,8},{8,12},{12,16},{16,20},{20,24},{24,28},{1,5},{5,9},{9,... | collective-permute-start | bytes 34568 | tf_op jit(solution)/shard_map/ppermute | solution.py:44
  203.5 11.1 %copy-start.24 = (f32[2,88,1440]{2,1,0:T(8,128)}, f32[2,88,1440]{2,1,0:T(8,128)S(1)}, u32[]{:S(2)}) copy-start(f32[2,88,1440]{2,1,0:T(8,128)S(1)} %fusion.54) | copy-start | bytes 3041284
  203.5 5.8 %collective-permute-start.13 = (f32[2,1,1440]{2,1,0:T(1,128)S(1)}, f32[2,1,1440]{2,1,0:T(1,128)S(1)}, u32[]{:S(2)}, u32[]{:S(2)}) collective-permute-start(f32[2,1,1440]{2,1,0:T(1,128)S(1)} %get-tuple-element.49), channel_id=1, source_target_pairs={{4,0},{8,4},{12,8},{16,12},{20,16},{24,20},{28,24},{0,28},{5,1},{9... | collective-permute-start | bytes 34568 | tf_op jit(solution)/shard_map/ppermute | solution.py:28
  207.9 6.4 %collective-permute-start.12 = (f32[2,1,1440]{2,1,0:T(1,128)S(1)}, f32[2,1,1440]{2,1,0:T(1,128)S(1)}, u32[]{:S(2)}, u32[]{:S(2)}) collective-permute-start(f32[2,1,1440]{2,1,0:T(1,128)S(1)} %get-tuple-element.48), channel_id=1, source_target_pairs={{0,4},{4,8},{8,12},{12,16},{16,20},{20,24},{24,28},{28,0},{1,5},{5... | collective-permute-start | bytes 34568 | tf_op jit(solution)/shard_map/ppermute | solution.py:26
  215.5 4.0 collective-permute-start.14
  215.5 4.2 collective-permute-start.15
  238.3 17.1 %collective-permute-start.19 = (f32[8,2,3,1440]{3,0,2,1:T(8,128)}, f32[8,2,3,1440]{3,0,2,1:T(8,128)S(1)}, u32[]{:S(2)}, u32[]{:S(2)}) collective-permute-start(f32[8,2,3,1440]{3,0,2,1:T(8,128)} %copy.46), channel_id=1, source_target_pairs={{4,0},{8,4},{12,8},{16,12},{20,16},{24,20},{28,24},{0,28},{5,1},{9... | collective-permute-start | bytes 829448 | tf_op jit(solution)/shard_map/ppermute | solution.py:28
  239.2 22.8 %collective-permute-start.18 = (f32[8,2,3,1440]{3,0,2,1:T(8,128)}, f32[8,2,3,1440]{3,0,2,1:T(8,128)}, u32[]{:S(2)}, u32[]{:S(2)}) collective-permute-start(f32[8,2,3,1440]{3,0,2,1:T(8,128)} %copy.45), channel_id=1, source_target_pairs={{0,4},{4,8},{8,12},{12,16},{16,20},{20,24},{24,28},{28,0},{1,5},{5... | collective-permute-start | bytes 829448 | tf_op jit(solution)/shard_map/ppermute | solution.py:26
  270.5 14.9 %collective-permute-start.21 = (f32[8,2,94,3]{2,0,3,1:T(8,128)S(1)}, f32[8,2,94,3]{2,0,3,1:T(8,128)S(1)}, u32[]{:S(2)}, u32[]{:S(2)}) collective-permute-start(f32[8,2,94,3]{2,0,3,1:T(8,128)S(1)} %get-tuple-element.21), channel_id=1, source_target_pairs={{1,0},{2,1},{3,2},{0,3},{5,4},{6,5},{7,6},{4,7},{9,8},{10,9},{11,1... | collective-permute-start | bytes 54152 | tf_op jit(solution)/shard_map/ppermute | solution.py:28
  271.8 13.6 %collective-permute-start.20 = (f32[8,2,94,3]{2,0,3,1:T(8,128)S(1)}, f32[8,2,94,3]{2,0,3,1:T(8,128)S(1)}, u32[]{:S(2)}, u32[]{:S(2)}) collective-permute-start(f32[8,2,94,3]{2,0,3,1:T(8,128)S(1)} %get-tuple-element.20), channel_id=1, source_target_pairs={{0,1},{1,2},{2,3},{3,0},{4,5},{5,6},{6,7},{7,4},{8,9},{9,10},{10,1... | collective-permute-start | bytes 54152 | tf_op jit(solution)/shard_map/ppermute | solution.py:26
  274.6 10.0 %copy-start.36 = (f32[1,2,88,1440]{3,2,1,0:T(8,128)S(1)}, f32[1,2,88,1440]{3,2,1,0:T(8,128)}, u32[]{:S(2)}) copy-start(f32[1,2,88,1440]{3,2,1,0:T(8,128)} %copy-done.35) | copy-start | bytes 3041284
  274.6 10.0 %copy-start.38 = (f32[1,2,88,1440]{3,2,1,0:T(8,128)S(1)}, f32[1,2,88,1440]{3,2,1,0:T(8,128)}, u32[]{:S(2)}) copy-start(f32[1,2,88,1440]{3,2,1,0:T(8,128)} %copy-done.37) | copy-start | bytes 3041284
  274.6 10.8 %slice-start = ((s8[11796480]{0:T(1024)(128)(4,1)}), s8[4194304]{0:T(1024)(128)(4,1)S(1)}, s32[]{:S(2)}) async-start(s8[11796480]{0:T(1024)(128)(4,1)} %bitcast.41), calls=%async_computation.3 | async-start | bytes 8388608
  274.6 10.8 %slice-start.1 = ((s8[11796480]{0:T(1024)(128)(4,1)}), s8[4194304]{0:T(1024)(128)(4,1)S(1)}, s32[]{:S(2)}) async-start(s8[11796480]{0:T(1024)(128)(4,1)} %bitcast.41), calls=%async_computation.4 | async-start | bytes 8388608
  285.2 18.3 %copy-start.29 = (f32[2,88,1440]{2,1,0:T(8,128)}, f32[2,88,1440]{2,1,0:T(8,128)S(1)}, u32[]{:S(2)}) copy-start(f32[2,88,1440]{2,1,0:T(8,128)S(1)} %get-tuple-element.29) | copy-start | bytes 3041284
  285.2 22.1 %copy-start.23 = (f32[2,88,1440]{2,1,0:T(8,128)}, f32[2,88,1440]{2,1,0:T(8,128)S(1)}, u32[]{:S(2)}) copy-start(f32[2,88,1440]{2,1,0:T(8,128)S(1)} %get-tuple-element.28) | copy-start | bytes 3041284
  285.3 22.0 %copy-start.20 = (f32[2,88,1440]{2,1,0:T(8,128)S(1)}, f32[2,88,1440]{2,1,0:T(8,128)}, u32[]{:S(2)}) copy-start(f32[2,88,1440]{2,1,0:T(8,128)} %copy-done.19) | copy-start | bytes 3041284
  285.3 22.0 %copy-start.22 = (f32[2,88,1440]{2,1,0:T(8,128)S(1)}, f32[2,88,1440]{2,1,0:T(8,128)}, u32[]{:S(2)}) copy-start(f32[2,88,1440]{2,1,0:T(8,128)} %copy-done.21) | copy-start | bytes 3041284
  285.3 22.0 %collective-permute-start.16 = (f32[2,88,1]{2,1,0:T(8,128)S(1)}, f32[2,88,1]{2,1,0:T(8,128)S(1)}, u32[]{:S(2)}, u32[]{:S(2)}) collective-permute-start(f32[2,88,1]{2,1,0:T(8,128)S(1)} %slice.368), channel_id=1, source_target_pairs={{0,1},{1,2},{2,3},{3,0},{4,5},{5,6},{6,7},{7,4},{8,9},{9,10},{10,1... | collective-permute-start | bytes 2120 | tf_op jit(solution)/shard_map/ppermute | solution.py:38
  303.6 53.2 %collective-permute-start.17 = (f32[2,1,1440]{2,1,0:T(1,128)S(1)}, f32[2,1,1440]{2,1,0:T(1,128)S(1)}, u32[]{:S(2)}, u32[]{:S(2)}) collective-permute-start(f32[2,1,1440]{2,1,0:T(1,128)S(1)} %slice.374), channel_id=1, source_target_pairs={{0,4},{4,8},{8,12},{12,16},{16,20},{20,24},{24,28},{1,5},{5,9},{9,... | collective-permute-start | bytes 34568 | tf_op jit(solution)/shard_map/ppermute | solution.py:44
  322.8 34.0 %copy-start.30 = (f32[2,88,1440]{2,1,0:T(8,128)S(1)}, f32[2,88,1440]{2,1,0:T(8,128)}, u32[]{:S(2)}) copy-start(f32[2,88,1440]{2,1,0:T(8,128)} %copy-done.29) | copy-start | bytes 3041284
  322.8 33.9 %copy-start.32 = (f32[2,88,1440]{2,1,0:T(8,128)S(1)}, f32[2,88,1440]{2,1,0:T(8,128)}, u32[]{:S(2)}) copy-start(f32[2,88,1440]{2,1,0:T(8,128)} %copy-done.31) | copy-start | bytes 3041284
  322.8 33.9 %copy-start.34 = (f32[2,88,1440]{2,1,0:T(8,128)S(1)}, f32[2,88,1440]{2,1,0:T(8,128)}, u32[]{:S(2)}) copy-start(f32[2,88,1440]{2,1,0:T(8,128)} %copy-done.33) | copy-start | bytes 3041284
  374.7 31.9 %copy-start.48 = (f32[2,88,1440]{1,2,0:T(8,128)S(1)}, f32[2,88,1440]{1,2,0:T(8,128)}, u32[]{:S(2)}) copy-start(f32[2,88,1440]{1,2,0:T(8,128)} %copy.27) | copy-start | bytes 3041284
  430.6 11.5 %copy-start.25 = (f32[2,88,1440]{2,1,0:T(8,128)S(1)}, f32[2,88,1440]{2,1,0:T(8,128)}, u32[]{:S(2)}) copy-start(f32[2,88,1440]{2,1,0:T(8,128)} %copy-done.24) | copy-start | bytes 3041284
  430.6 11.5 %copy-start.39 = (f32[2,88,1441]{2,1,0:T(8,128)S(1)}, f32[2,88,1441]{2,1,0:T(8,128)}, u32[]{:S(2)}) copy-start(f32[2,88,1441]{2,1,0:T(8,128)} %get-tuple-element.15) | copy-start | bytes 3043396
  (37 other events, 72.0 us)
Sparse Core Ops, SparseCore 0:
  51.2 42.6 all-reduce.3
  145.9 38.3 all-reduce.5
  236.0 38.5 all-reduce.7
where the time goes:
time: 461 us; the launch traced here: 452 us
  other arithmetic  152 us (33%)
  waiting for transfers between devices  103 us (22%)
  local copies, waits for them, and re-layouts  91.6 us (20%)
  matrix products  54.8 us (12%)
  starting transfers between devices  35.8 us (8%)
  between operations  14.7 us (3%)
    psum x3, waiting for transfers between devices, spectral_filter(): lax.psum(partial_sums, 'lon') * spectral_weights(flat_cut, NLON, KMAX)  81.5 us
    unnamed x125, local copies, waits for them, and re-layouts  46.2 us
    mul x1, other arithmetic, local(): carried_x = mass_x * faces_x  33.9 us
    mul x1, other arithmetic, local(): carried_y = mass_y * faces_y  31.9 us
    dot_general x3, matrix products, spectral_filter(): jnp.dot(coeffs, basis.T, precision=lax.Precision.HIGHEST, preferred_eleme...  30 us
    dot_general x3, matrix products, spectral_filter(): jnp.dot(flat, basis, precision=lax.Precision.HIGHEST, preferred_element_t...  24.8 us
    sub x1, other arithmetic, local(): tracers * thickness  23.9 us
    ppermute x8, starting transfers between devices, padded_2(): lax.ppermute(head, axis, [((i + 1) % count, i) for i in range(count)])  22.1 us
  transfers between devices with their start and end apart: 25, of which 17 were waited for; matrix products, arithmetic and copies ran while one was open for 28% of the time, Pallas kernels for 0%

commit v1 on v0

v1 whole, which is shorter than its diff:
```python
import math

import numpy as np
import jax
import jax.numpy as jnp
from jax import lax
from jax.experimental import pallas as pl
from jax.experimental.pallas import tpu as pltpu
from jax.sharding import PartitionSpec as P

NLON = 5760
KMAX = 512
SUBSTEPS = 3

LAT_EDGE = 85.0 * math.pi / 180.0
PRESSURE_PUSH = 0.08
DIVERGE_RATE = 0.08
COURANT_RATE = 0.3

HALO = 3
SOUTH_PAD = 4
SIDE = 8
VMEM_LIMIT = 56 * 1024 * 1024


def center_cos(global_rows, total_rows):
    return jnp.cos(((2 * global_rows + 1).astype(jnp.float32) / total_rows - 1.0) * LAT_EDGE)


def face_cos(global_rows, total_rows):
    return jnp.cos(((2 * global_rows + 2).astype(jnp.float32) / total_rows - 1.0) * LAT_EDGE)


def shifted(array, axis, by, wrap):
    count = lax.axis_size(axis)
    pairs = [(i, (i + by) % count) for i in range(count) if wrap or 0 <= i + by < count]
    return lax.ppermute(array, axis, pairs)


def split_bf16(values):
    high = values.astype(jnp.bfloat16)
    low = (values - high.astype(jnp.float32)).astype(jnp.bfloat16)
    return high, low


def basis_tables(width, lanes):
    lane = np.arange(lanes)
    column = np.where(lane < (width + lanes) // 2, lane, lane - lanes)
    phase = (column[:, None] * np.arange(KMAX)[None, :]) % NLON
    angle = phase * (2.0 * math.pi / NLON)
    full = np.concatenate([np.cos(angle), np.sin(angle)], axis=1).astype(np.float32)
    own = np.where((lane < width)[:, None], full, np.float32(0))

    def parts(table):
        high = table.astype(jnp.bfloat16)
        low = (table - high.astype(np.float32)).astype(jnp.bfloat16)
        return jnp.asarray(high), jnp.asarray(low)

    return parts(own), parts(np.ascontiguousarray(full.T))


def dot3(values, high_ref, low_ref):
    high, low = split_bf16(values)
    return (
        jnp.dot(high, high_ref[...], preferred_element_type=jnp.float32)
        + jnp.dot(low, high_ref[...], preferred_element_type=jnp.float32)
        + jnp.dot(high, low_ref[...], preferred_element_type=jnp.float32)
    )


def ahead(values, axis):
    return pltpu.roll(values, values.shape[axis] - 1, axis)


def behind(values, axis):
    return pltpu.roll(values, 1, axis)


def push_winds(p, u, v, rows):
    u = u - rows[:, 0:1] * (ahead(p, 1) - p)
    v = (v - PRESSURE_PUSH * (ahead(p, 0) - p)) * rows[:, 1:2]
    return u, v


def edge_columns(first, last, width):
    end = width % 128
    return first.T[:SIDE], last.T[end - SIDE : end]


def side_lanes(east, west, width):
    end = width % 128
    rows = east.shape[1]
    fill = jnp.zeros((end, rows), jnp.float32)
    gap = jnp.zeros((128 - end - 2 * SIDE, rows), jnp.float32)
    return jnp.concatenate([fill, east, gap, west], axis=0).T


def tracer_edges(width, first_ref, last_ref, head_out, tail_out):
    for t in range(first_ref.shape[0]):
        for l in range(first_ref.shape[1]):
            head, tail = edge_columns(first_ref[t, l], last_ref[t, l], width)
            head_out[t, l] = head
            tail_out[t, l] = tail


def field_edges(width, *refs):
    fields, (south, north), (head_out, tail_out, block) = refs[:6], (refs[6:8], refs[8:10]), refs[10:]
    levels, own_rows = fields[0].shape[:2]
    for f in range(3):
        for l in range(levels):
            sides = []
            for end in range(2):
                block[...] = jnp.zeros_like(block)
                block[SOUTH_PAD - HALO : SOUTH_PAD] = south[end][f, l]
                block[SOUTH_PAD : SOUTH_PAD + own_rows] = fields[2 * f + end][l]
                block[SOUTH_PAD + own_rows : SOUTH_PAD + own_rows + HALO] = north[end][f, l]
                sides.append(block[...])
            head, tail = edge_columns(sides[0], sides[1], width)
            head_out[f, l] = head
            tail_out[f, l] = tail


def first_kernel(
    width, p_ref, u_ref, v_ref, south_ref, north_ref, east_ref, west_ref, rows_ref, fh_ref, fl_ref,
    p_out, u_out, v_out, sums_out, ext
):
    own_rows = p_ref.shape[1]
    whole = width // 128 * 128
    wide = []
    for at, ref in enumerate((p_ref, u_ref, v_ref)):
        ext[at] = jnp.zeros(ext.shape[1:], jnp.float32)
        ext[at, SOUTH_PAD - HALO : SOUTH_PAD, :width] = south_ref[at, 0]
        ext[at, SOUTH_PAD : SOUTH_PAD + own_rows, :width] = ref[0]
        ext[at, SOUTH_PAD + own_rows : SOUTH_PAD + own_rows + HALO, :width] = north_ref[at, 0]
        ext[at, :, whole:] = ext[at, :, whole:] + side_lanes(east_ref[at, 0], west_ref[at, 0], width)
        wide.append(ext[at])
    p_out[0] = wide[0]
    u, v = push_winds(*wide, rows_ref[...])
    u_out[0] = u
    v_out[0] = v
    sums_out[0] = dot3(jnp.concatenate([u, v], axis=0), fh_ref, fl_ref)


def step_kernel(first, last, *refs):
    p_ref, u_ref, v_ref, coeff_ref, rows_ref, ih_ref, il_ref = refs[:7]
    refs = refs[7:]
    if not last:
        fh_ref, fl_ref = refs[:2]
        refs = refs[2:]
    if not first:
        sums_in = refs[:4]
        refs = refs[4:]
    sums_out = refs[:4]
    p_out, u_out, v_out = refs[4:7]
    rows = rows_ref[...]
    count = rows.shape[0]
    smooth = dot3(coeff_ref[0], ih_ref, il_ref)
    polar = rows[:, 3:4] > 0.0
    p = p_ref[0]
    u = jnp.where(polar, smooth[:count], u_ref[0])
    v = jnp.where(polar, smooth[count:], v_ref[0])
    flux_x = 0.5 * (p + ahead(p, 1)) * u
    flux_y = (p + ahead(p, 0)) * v * rows[:, 2:3]
    p = p - rows[:, 0:1] * ((flux_x - behind(flux_x, 1)) + (flux_y - behind(flux_y, 0)))
    for at, term in enumerate((flux_x, flux_y, u, v)):
        sums_out[at][0] = term if first else sums_in[at][0] + term
    if last:
        own = slice(SOUTH_PAD, SOUTH_PAD + p_out.shape[1])
        width = p_out.shape[2]
        p_out[0] = p[own, :width]
        u_out[0] = u[own, :width]
        v_out[0] = v[own, :width]
    else:
        p_out[0] = p
        u, v = push_winds(p, u, v, rows)
        u_out[0] = u
        v_out[0] = v
        refs[7][0] = dot3(p, fh_ref, fl_ref)


def tracer_kernel(
    own_rows, width, q_ref, east_ref, west_ref, south_ref, north_ref, thick_ref, fx_ref, fy_ref, ua_ref, va_ref, rows_ref,
    out_ref, ext, edge, flux, cx, xa, xe, xq, cy, ya, ye, yq, row_k
):
    lanes = ext.shape[1]
    whole = width // 128 * 128
    ext_rows = rows_ref.shape[0]

    @pl.when(pl.program_id(1) == 0)
    def _():
        def coefficients(mass, courant):
            size = jnp.abs(courant)
            slope = mass * size * 0.5
            curve = slope * (1.0 - size * (2.0 / 3.0))
            near = (mass - slope - 3.0 * curve) * (1.0 / 12.0)
            far = (slope - 3.0 * curve) * (1.0 / 12.0)
            return near, far, 6.0 * curve

        own = pl.ds(SOUTH_PAD, own_rows)
        k = rows_ref[own, 0:1]
        c = jnp.clip(rows_ref[own, 4:5] * ua_ref[0, own, :], -1.0, 1.0)
        cx[...] = c
        near, far, cell = coefficients(fx_ref[0, own, :] * k, c)
        xa[...] = near
        xe[...] = far
        xq[...] = cell
        faces = pl.ds(SOUTH_PAD - 1, own_rows + 1)
        at = pl.ds(0, own_rows + 1)
        c = jnp.clip(COURANT_RATE * va_ref[0, faces, :], -1.0, 1.0)
        cy[at, :] = c
        near, far, cell = coefficients(fy_ref[0, faces, :], c)
        ya[at, :] = near
        ye[at, :] = far
        yq[at, :] = cell
        row_k[...] = jnp.broadcast_to(k, row_k.shape)

    ext[8 - HALO : 8, 0:width] = south_ref[0, 0]
    ext[8 + own_rows : 8 + own_rows + HALO, 0:width] = north_ref[0, 0]
    ext[8 : 8 + own_rows, 0:width] = q_ref[0, 0]
    tail = ext[8 : 8 + own_rows, whole:lanes]
    sides = side_lanes(east_ref[0, 0], west_ref[0, 0], width)
    lane = lax.broadcasted_iota(jnp.int32, tail.shape, 1)
    ext[8 : 8 + own_rows, whole:lanes] = jnp.where(lane < width - whole, tail, sides)

    for at in range(0, own_rows, 8):
        here = slice(at, at + 8)
        q = ext[8 + at : 16 + at, :]
        q_next = ahead(q, 1)
        a = 7.0 * (q + q_next) - (behind(q, 1) + pltpu.roll(q, lanes - 2, 1))
        positive = cx[here, :] > 0.0
        e = jnp.where(positive, behind(a, 1), ahead(a, 1))
        cell = jnp.where(positive, q, q_next)
        f = xa[here, :] * a + xe[here, :] * e + xq[here, :] * cell
        f = f - behind(f, 1)
        out_ref[0, 0, here, :] = q[:, :width] * thick_ref[0, here, :] - f[:, :width]

    span = own_rows + 8
    for at in range(0, width, 128):
        here = slice(at, min(at + 128, width))

        edge[0:span, here] = 7.0 * (
            ext[6 : 6 + span, here] + ext[7 : 7 + span, here]
        ) - (ext[5 : 5 + span, here] + ext[8 : 8 + span, here])
        n = own_rows + 1
        positive = cy[0:n, here] > 0.0
        e = jnp.where(positive, edge[0:n, here], edge[2 : 2 + n, here])
        cell = jnp.where(positive, ext[7 : 7 + n, here], ext[8 : 8 + n, here])
        flux[0:n, here] = (
            ya[0:n, here] * edge[1 : 1 + n, here] + ye[0:n, here] * e + yq[0:n, here] * cell
        )
        change = flux[1:n, here] - flux[0 : n - 1, here]
        k = row_k[:, : here.stop - here.start]
        out_ref[0, 0, :, here] = out_ref[0, 0, :, here] - k * change


def circle_sums(partial):
    count = lax.axis_size("lon")
    if count != 4 or partial.shape[0] != 2:
        return lax.psum(partial, "lon")
    even = lax.axis_index("lon") % 2 == 0
    sibling = [(i, i ^ 1) for i in range(count)]
    across = [(i, i ^ 2) for i in range(count)]
    kept = jnp.where(even, partial[0], partial[1])
    sent = jnp.where(even, partial[1], partial[0])
    half = kept + lax.ppermute(sent, "lon", sibling)
    half = half + lax.ppermute(half, "lon", across)
    other = lax.ppermute(half, "lon", sibling)
    return jnp.stack([jnp.where(even, half, other), jnp.where(even, other, half)])


def local(thickness, zonal_wind, merid_wind, tracers, cutoffs):
    levels, own_rows, width = thickness.shape
    tracer_count = tracers.shape[0]
    total_rows = own_rows * lax.axis_size("lat")
    lanes = (width // 128 + 1) * 128
    ext_rows = own_rows + 8
    f32 = jnp.float32

    whole = width // 128 * 128
    q_south = shifted(tracers[:, :, -HALO:], "lat", 1, False)
    q_north = shifted(tracers[:, :, :HALO], "lat", -1, False)
    south = shifted(
        jnp.stack([x[:, -HALO:] for x in (thickness, zonal_wind, merid_wind)]), "lat", 1, False
    )
    north = shifted(
        jnp.stack([x[:, :HALO] for x in (thickness, zonal_wind, merid_wind)]), "lat", -1, False
    )
    q_block = (tracer_count, levels, own_rows, 128)
    q_side = jax.ShapeDtypeStruct((tracer_count, levels, SIDE, own_rows), f32)
    q_head, q_tail = pl.pallas_call(
        lambda *refs: tracer_edges(width, *refs),
        grid=(1,),
        in_specs=[
            pl.BlockSpec(q_block, lambda i: (0, 0, 0, 0)),
            pl.BlockSpec(q_block, lambda i: (0, 0, 0, whole // 128)),
        ],
        out_specs=[pl.BlockSpec(q_side.shape, lambda i: (0, 0, 0, 0))] * 2,
        out_shape=[q_side] * 2,
        name="tracer_edges",
    )(tracers, tracers)
    q_west = shifted(q_tail, "lon", 1, True)
    q_east = shifted(q_head, "lon", -1, True)

    side = jax.ShapeDtypeStruct((3, levels, SIDE, ext_rows), f32)
    own_block, cap_block = (levels, own_rows, 128), (3, levels, HALO, 128)
    ends = [0, whole // 128]
    head, tail = pl.pallas_call(
        lambda *refs: field_edges(width, *refs),
        grid=(1,),
        in_specs=[pl.BlockSpec(own_block, lambda i, e=e: (0, 0, e)) for _ in range(3) for e in ends]
        + [pl.BlockSpec(cap_block, lambda i, e=e: (0, 0, 0, e)) for _ in range(2) for e in ends],
        out_specs=[pl.BlockSpec(side.shape, lambda i: (0, 0, 0, 0))] * 2,
        out_shape=[side] * 2,
        scratch_shapes=[pltpu.VMEM((ext_rows, 128), f32)],
        name="field_edges",
    )(
        thickness, thickness, zonal_wind, zonal_wind, merid_wind, merid_wind,
        south, south, north, north,
    )
    west = shifted(tail, "lon", 1, True)
    east = shifted(head, "lon", -1, True)

    global_rows = (
        lax.axis_index("lat") * own_rows - SOUTH_PAD + jnp.arange(ext_rows, dtype=jnp.int32)
    )
    cos_center = center_cos(global_rows, total_rows)
    wall = ((global_rows >= 0) & (global_rows < total_rows - 1)).astype(f32)
    polar = total_rows // 8
    is_polar = ((global_rows >= 0) & (global_rows < polar)) | (
        (global_rows >= total_rows - polar) & (global_rows < total_rows)
    )
    rate = DIVERGE_RATE / cos_center
    columns = [
        rate, wall, 0.5 * face_cos(global_rows, total_rows) * wall, is_polar.astype(f32),
        COURANT_RATE / cos_center,
    ]
    rows = jnp.pad(jnp.stack(columns, axis=1), ((0, 0), (0, 128 - len(columns))))
    slot = jnp.where(global_rows < polar, global_rows, global_rows - total_rows + 2 * polar)
    matches = slot[:, None] == jnp.arange(2 * polar, dtype=jnp.int32)[None, :]
    row_cut = jnp.sum(jnp.where(matches, cutoffs[None, :], 0), axis=1)
    waves = jnp.arange(KMAX, dtype=jnp.int32)
    scaled = jnp.where(waves == 0, 1.0, 2.0).astype(f32) / NLON
    weight = jnp.where(waves[None, :] < row_cut[:, None], scaled[None, :], 0.0)

    step_angle = 2.0 * math.pi / NLON
    phase = (lax.axis_index("lon") * width * waves) % NLON
    turn_cos = jnp.cos(phase.astype(f32) * step_angle)
    turn_sin = jnp.sin(phase.astype(f32) * step_angle)

    def summed(partial):
        a, b = partial[..., :KMAX], partial[..., KMAX:]
        partial = jnp.concatenate(
            [a * turn_cos - b * turn_sin, a * turn_sin + b * turn_cos], axis=-1
        )
        total = circle_sums(partial)
        a, b = total[..., :KMAX], total[..., KMAX:]
        return a * turn_cos + b * turn_sin, b * turn_cos - a * turn_sin

    wave_angle = waves.astype(f32) * step_angle
    next_sin = jnp.sin(wave_angle)
    next_less = -2.0 * jnp.sin(0.5 * wave_angle) ** 2

    (fh, fl), (ih, il) = basis_tables(width, lanes)
    wide_shape = jax.ShapeDtypeStruct((levels, ext_rows, lanes), f32)
    wide_spec = pl.BlockSpec((1, ext_rows, lanes), lambda l: (l, 0, 0))
    once = pl.Buffered(1)
    rows_spec = pl.BlockSpec(rows.shape, lambda l: (0, 0))
    f_spec = pl.BlockSpec(fh.shape, lambda l: (0, 0), pipeline_mode=once)
    i_spec = pl.BlockSpec(ih.shape, lambda l: (0, 0), pipeline_mode=once)
    params = pltpu.CompilerParams(
        dimension_semantics=("arbitrary",), vmem_limit_bytes=VMEM_LIMIT
    )

    def sums_of(count):
        return (
            jax.ShapeDtypeStruct((levels, count, 2 * KMAX), f32),
            pl.BlockSpec((1, count, 2 * KMAX), lambda l: (l, 0, 0)),
        )

    sums_shape, sums_spec = sums_of(2 * ext_rows)
    p_shape, p_spec = sums_of(ext_rows)
    own_spec = pl.BlockSpec((1, own_rows, width), lambda l: (l, 0, 0))
    own_shape = jax.ShapeDtypeStruct((levels, own_rows, width), f32)
    cap_spec = pl.BlockSpec((3, 1, HALO, width), lambda l: (0, l, 0, 0))
    side_spec = pl.BlockSpec((3, 1, SIDE, ext_rows), lambda l: (0, l, 0, 0))
    p, u, v, partial = pl.pallas_call(
        lambda *refs: first_kernel(width, *refs),
        grid=(levels,),
        in_specs=[own_spec] * 3 + [cap_spec] * 2 + [side_spec] * 2 + [rows_spec, f_spec, f_spec],
        out_specs=[wide_spec] * 3 + [sums_spec],
        out_shape=[wide_shape] * 3 + [sums_shape],
        scratch_shapes=[pltpu.VMEM((3, ext_rows, lanes), f32)],
        compiler_params=params,
        name="first_push",
    )(thickness, zonal_wind, merid_wind, south, north, east, west, rows, fh, fl)

    a, b = summed(partial)
    a = a.reshape(levels, 2, ext_rows, KMAX) * weight
    b = b.reshape(levels, 2, ext_rows, KMAX) * weight
    ua, va, ub, vb = a[:, 0], a[:, 1], b[:, 0], b[:, 1]
    sums = ()
    for substep in range(SUBSTEPS):
        first, last = substep == 0, substep == SUBSTEPS - 1
        coeffs = jnp.concatenate(
            [jnp.concatenate([ua, ub], axis=-1), jnp.concatenate([va, vb], axis=-1)], axis=1
        )
        ins = [p, u, v, coeffs, rows, ih, il]
        in_specs = [wide_spec] * 3 + [sums_spec, rows_spec, i_spec, i_spec]
        if not last:
            ins += [fh, fl]
            in_specs += [f_spec, f_spec]
        ins += list(sums)
        in_specs += [wide_spec] * len(sums)
        out_shape = [wide_shape] * 4 + ([own_shape] * 3 if last else [wide_shape] * 3 + [p_shape])
        out_specs = [wide_spec] * 4 + ([own_spec] * 3 if last else [wide_spec] * 3 + [p_spec])

        def body(*refs, first=first, last=last):
            step_kernel(first, last, *refs)

        outs = pl.pallas_call(
            body,
            grid=(levels,),
            in_specs=in_specs,
            out_specs=out_specs,
            out_shape=out_shape,
            compiler_params=params,
            name="substep",
        )(*ins)
        sums = outs[:4]
        p, u, v = outs[4:7]
        if not last:
            pa, pb = summed(outs[7])
            da = next_less * pa + next_sin * pb
            db = next_less * pb - next_sin * pa
            push_u = rate[:, None] * (PRESSURE_PUSH / DIVERGE_RATE) * weight
            push_v = PRESSURE_PUSH * weight
            ua, ub = ua - push_u * da, ub - push_u * db
            va = (va - push_v * (jnp.roll(pa, -1, axis=1) - pa)) * wall[:, None]
            vb = (vb - push_v * (jnp.roll(pb, -1, axis=1) - pb)) * wall[:, None]

    acc_spec = pl.BlockSpec((1, ext_rows, lanes), lambda l, t: (l, 0, 0))
    tracer_mass = pl.pallas_call(
        lambda *refs: tracer_kernel(own_rows, width, *refs),
        grid=(levels, tracer_count),
        in_specs=[
            pl.BlockSpec((1, 1, own_rows, width), lambda l, t: (t, l, 0, 0)),
            pl.BlockSpec((1, 1, SIDE, own_rows), lambda l, t: (t, l, 0, 0)),
            pl.BlockSpec((1, 1, SIDE, own_rows), lambda l, t: (t, l, 0, 0)),
            pl.BlockSpec((1, 1, HALO, width), lambda l, t: (t, l, 0, 0)),
            pl.BlockSpec((1, 1, HALO, width), lambda l, t: (t, l, 0, 0)),
            pl.BlockSpec((1, own_rows, width), lambda l, t: (l, 0, 0)),
            acc_spec, acc_spec, acc_spec, acc_spec,
            pl.BlockSpec(rows.shape, lambda l, t: (0, 0)),
        ],
        out_specs=pl.BlockSpec((1, 1, own_rows, width), lambda l, t: (t, l, 0, 0)),
        out_shape=jax.ShapeDtypeStruct(tracers.shape, f32),
        scratch_shapes=[pltpu.VMEM((own_rows + 16, lanes), f32)]
        + [pltpu.VMEM((own_rows + 16, lanes), f32)] * 2
        + [pltpu.VMEM((own_rows, lanes), f32)] * 4
        + [pltpu.VMEM((own_rows + 8, lanes), f32)] * 4
        + [pltpu.VMEM((own_rows, 128), f32)],
        compiler_params=pltpu.CompilerParams(
            dimension_semantics=("arbitrary", "arbitrary"), vmem_limit_bytes=VMEM_LIMIT
        ),
        name="tracers",
    )(tracers, q_east, q_west, q_south, q_north, thickness, *sums, rows)

    return (p, u, v, tracer_mass)


def solution(mesh):
    return jax.shard_map(
        local,
        mesh=mesh,
        in_specs=(
            P(None, "lat", "lon"),
            P(None, "lat", "lon"),
            P(None, "lat", "lon"),
            P(None, None, "lat", "lon"),
            P(),
        ),
        out_specs=(
            P(None, "lat", "lon"),
            P(None, "lat", "lon"),
            P(None, "lat", "lon"),
            P(None, None, "lat", "lon"),
        ),
        check_vma=False,
    )
```

time: 461 us -> 192 us (0.42); the launches traced: 452 us -> 191 us
  other arithmetic: 152 us -> 11.2 us
  Pallas kernels: 0 us -> 97.3 us
  local copies, waits for them, and re-layouts: 91.6 us -> 6.8 us
  matrix products: 54.8 us -> 0 us
  waiting for transfers between devices: 103 us -> 54.9 us
  starting transfers between devices: 35.8 us -> 20.1 us
  between operations: 14.7 us -> 1.12 us
    pallas_call x0 -> x7, Pallas kernels: none -> 97.3 us  [the longest x1 41.9 us: local(): pl.pallas_call(lambda *refs: tracer_kernel(own_rows, width, *refs), grid=...]
    psum x3 -> x0, waiting for transfers between devices: 81.5 us -> none  [spectral_filter(): lax.psum(partial_sums, 'lon') * spectral_weights(flat_cut, NLON, KMAX)]
    mul x8 -> x3, other arithmetic: 71.7 us -> 0.41 us  [the longest x1 0.24 us: local(): a = a.reshape(levels, 2, ext_rows, KMAX) * weight]
    dot_general x6 -> x0, matrix products: 54.8 us -> none  [the longest x3 30 us: spectral_filter(): jnp.dot(coeffs, basis.T, precision=lax.Precision.HIGHEST, preferred_eleme...]
    unnamed x125 -> x18, local copies, waits for them, and re-layouts: 46.2 us -> 2.23 us
    ppermute x22 -> x17, waiting for transfers between devices: 21 us -> 54.9 us  [the longest x3 38.1 us: circle_sums(): half = half + lax.ppermute(half, 'lon', across)]
    select_n x9 -> x4, other arithmetic: 23.1 us -> 0.2 us  [the longest x3 0.19 us: circle_sums(): sent = jnp.where(even, partial[1], partial[0])]
    sub x4 -> x7, other arithmetic: 28.1 us -> 5.24 us  [the longest x3 4.06 us: summed(): a * turn_cos - b * turn_sin]
  transfers between devices with their start and end apart: 25 -> 17, of which waited for: 17 -> 12; matrix products, arithmetic and copies ran while one was open for 28% -> 3% of each run, Pallas kernels for 0% -> 7%
where the time goes in v1:
time: 192 us; the launch traced here: 191 us
  Pallas kernels  97.3 us (51%)
  waiting for transfers between devices  54.9 us (29%)
  starting transfers between devices  20.1 us (10%)
  other arithmetic  11.2 us (6%)
  local copies, waits for them, and re-layouts  6.8 us (4%)
    pallas_call x1, Pallas kernels, local(): pl.pallas_call(lambda *refs: tracer_kernel(own_rows, width, *refs), grid=...  41.9 us
    pallas_call x3, Pallas kernels, local(): pl.pallas_call(body, grid=(levels,), in_specs=in_specs, out_specs=out_spe...  41.5 us
    ppermute x3, waiting for transfers between devices, circle_sums(): half = half + lax.ppermute(half, 'lon', across)  38.1 us
    ppermute x8, starting transfers between devices, shifted(): return lax.ppermute(array, axis, pairs)  15.5 us
    pallas_call x1, Pallas kernels, local(): pl.pallas_call(lambda *refs: first_kernel(width, *refs), grid=(levels,),...  9.53 us
    ppermute x8, waiting for transfers between devices, shifted(): return lax.ppermute(array, axis, pairs)  7.66 us
    ppermute x3, waiting for transfers between devices, circle_sums(): half = kept + lax.ppermute(sent, 'lon', sibling)  5.46 us
    sub x3, other arithmetic, summed(): a * turn_cos - b * turn_sin  4.06 us
  transfers between devices with their start and end apart: 17, of which 12 were waited for; matrix products, arithmetic and copies ran while one was open for 3% of the time, Pallas kernels for 7%

profile of v1, /device:TPU:0, one launch (start us, length us, event | category | flops | bytes accessed | tf_op | source)
XLA Modules:
  0.0 191.4 jit_solution(15348212727379859559)
XLA Ops:
  0.6 1.0 slice_bitcast_fusion.6
  1.6 1.1 slice_bitcast_fusion.4
  2.7 1.3 collective-permute-start.1
  4.1 5.5 %collective-permute-start = (f32[3,2,3,1440]{3,2,1,0:T(4,128)S(1)}, f32[3,2,3,1440]{3,2,1,0:T(4,128)S(1)}, u32[]{:S(2)}, u32[]{:S(2)}) collective-permute-start(f32[3,2,3,1440]{3,2,1,0:T(4,128)S(1)} %pad_maximum_fusion.6), channel_id=1, source_target_pairs={{0,4},{4,8},{8,12},{12,16},{16,20},{20,24},{24,28},{1,5},{5,9},{9,... | collective-permute-start | bytes 311048 | tf_op jit(solution)/shard_map/ppermute | solution.py:37
  9.7 1.7 collective-permute-done.1.refs_8_.refs_9_.refs_4_
  11.4 3.3 %collective-permute-done.refs_6_.refs_7_.refs_3_ = f32[3,2,3,1440]{3,2,1,0:T(4,128)S(1)} collective-permute-done((f32[3,2,3,1440]{3,2,1,0:T(4,128)S(1)}, f32[3,2,3,1440]{3,2,1,0:T(4,128)S(1)}, u32[]{:S(2)}, u32[]{:S(2)}) %collective-permute-start) | collective-permute-done | bytes 103712 | tf_op jit(solution)/shard_map/ppermute | solution.py:37
  14.7 0.7 copy-done.1
  15.4 2.0 %field_edges.1 = (f32[3,2,8,96]{3,2,1,0:T(8,128)}, f32[3,2,8,96]{3,2,1,0:T(8,128)}) custom-call(f32[2,88,1440]{2,1,0:T(8,128)} %refs_5_.6, f32[2,88,1440]{2,1,0:T(8,128)} %refs_5_.6, f32[2,88,1440]{2,1,0:T(8,128)} %refs_1_.4, f32[2,88,1440]{2,1,0:T(8,128)} %refs_1_.4, f32[2,88,1440]{2,1,0:T(8,128)} %refs_2_.3, f32[2,88,1440]{2,1,0:T(8,128)} %refs_2_.3, ...), custom_call_target="tpu_custom_call" | custom-call | tf_op jit(solution)/shard_map/field_edges/pallas_call | solution.py:307
  17.4 1.1 collective-permute-start.2
  18.7 0.6 pad.4.refs_7_.refs_4_.refs_10_
  19.3 1.0 collective-permute-done.2.refs_5_
  20.3 1.7 collective-permute-done.3.refs_6_
  22.0 0.6 copy-done.5
  22.6 9.5 %first_push.1 = (f32[2,96,1536]{2,1,0:T(8,128)}, f32[2,96,1536]{2,1,0:T(8,128)}, f32[2,96,1536]{2,1,0:T(8,128)}, f32[2,192,1024]{2,1,0:T(8,128)}) custom-call(f32[2,88,1440]{2,1,0:T(8,128)} %refs_5_.6, f32[2,88,1440]{2,1,0:T(8,128)} %refs_1_.4, f32[2,88,1440]{2,1,0:T(8,128)} %refs_2_.3, f32[3,2,3,1440]{3,2,1,0:T(4,128)} %copy-done.1, ...), custom_call_target="tpu_custom_call" | custom-call | tf_op jit(solution)/shard_map/first_push/pallas_call | solution.py:386
  32.1 1.6 multiply_subtract_fusion.1
  33.9 2.3 %collective-permute-done.4 = f32[192,1024]{1,0:T(8,128)S(1)} collective-permute-done((f32[192,1024]{1,0:T(8,128)S(1)}, f32[192,1024]{1,0:T(8,128)S(1)}, u32[]{:S(2)}, u32[]{:S(2)}) %collective-permute-start.4) | collective-permute-done | bytes 786464 | tf_op jit(solution)/shard_map/ppermute | solution.py:265
  36.4 1.2 collective-permute-start.5
  37.5 18.5 %collective-permute-done.5 = f32[192,1024]{1,0:T(8,128)S(1)} collective-permute-done((f32[192,1024]{1,0:T(8,128)S(1)}, f32[192,1024]{1,0:T(8,128)S(1)}, u32[]{:S(2)}, u32[]{:S(2)}) %collective-permute-start.5) | collective-permute-done | bytes 786464 | tf_op jit(solution)/shard_map/ppermute | solution.py:266
  56.5 2.0 %collective-permute-done.6 = f32[192,1024]{1,0:T(8,128)S(1)} collective-permute-done((f32[192,1024]{1,0:T(8,128)S(1)}, f32[192,1024]{1,0:T(8,128)S(1)}, u32[]{:S(2)}, u32[]{:S(2)}) %collective-permute-start.6) | collective-permute-done | bytes 786464 | tf_op jit(solution)/shard_map/ppermute | solution.py:267
  58.7 0.2 multiply_add_fusion
  58.9 0.2 copy_multiply_fusion.1
  59.3 1.3 maximum_maximum_fusion.refs_3_
  60.6 14.5 %substep.3 = (f32[2,96,1536]{2,1,0:T(8,128)}, f32[2,96,1536]{2,1,0:T(8,128)}, f32[2,96,1536]{2,1,0:T(8,128)}, f32[2,96,1536]{2,1,0:T(8,128)}, f32[2,96,1536]{2,1...) custom-call(f32[2,96,1536]{2,1,0:T(8,128)} %get-tuple-element.37.refs_0_, ...), custom_call_target="tpu_custom_call" | custom-call | tf_op jit(solution)/shard_map/substep/pallas_call | solution.py:420
  75.0 1.2 multiply_subtract_fusion.9
  76.3 0.2 collective-permute-start.7
  76.5 1.6 collective-permute-done.7
  78.2 1.4 collective-permute-start.8
  79.6 9.8 %collective-permute-done.8 = f32[96,1024]{1,0:T(8,128)S(1)} collective-permute-done((f32[96,1024]{1,0:T(8,128)S(1)}, f32[96,1024]{1,0:T(8,128)S(1)}, u32[]{:S(2)}, u32[]{:S(2)}) %collective-permute-start.8) | collective-permute-done | bytes 393248 | tf_op jit(solution)/shard_map/ppermute | solution.py:266
  89.6 1.6 collective-permute-done.9
  91.6 0.4 multiply_subtract_fusion.6
  92.0 1.3 maximum_maximum_fusion.1.refs_3_
  93.3 15.6 %substep.4 = (f32[2,96,1536]{2,1,0:T(8,128)}, f32[2,96,1536]{2,1,0:T(8,128)}, f32[2,96,1536]{2,1,0:T(8,128)}, f32[2,96,1536]{2,1,0:T(8,128)}, f32[2,96,1536]{2,1...) custom-call(f32[2,96,1536]{2,1,0:T(8,128)} %get-tuple-element.41.refs_0_, ...), custom_call_target="tpu_custom_call" | custom-call | tf_op jit(solution)/shard_map/substep/pallas_call | solution.py:420
  108.9 1.2 multiply_subtract_fusion.5
  110.2 0.2 collective-permute-start.10
  110.4 1.6 collective-permute-done.10
  112.0 1.4 collective-permute-start.11
  113.4 9.8 %collective-permute-done.11 = f32[96,1024]{1,0:T(8,128)S(1)} collective-permute-done((f32[96,1024]{1,0:T(8,128)S(1)}, f32[96,1024]{1,0:T(8,128)S(1)}, u32[]{:S(2)}, u32[]{:S(2)}) %collective-permute-start.11) | collective-permute-done | bytes 393248 | tf_op jit(solution)/shard_map/ppermute | solution.py:266
  123.4 1.5 fusion.31
  124.9 5.1 %collective-permute-start.15 = (f32[8,2,3,1440]{3,2,1,0:T(4,128)S(1)}, f32[8,2,3,1440]{3,2,1,0:T(4,128)}, u32[]{:S(2)}, u32[]{:S(2)}) collective-permute-start(f32[8,2,3,1440]{3,2,1,0:T(4,128)S(1)} %get-tuple-element.73), channel_id=1, source_target_pairs={{0,4},{4,8},{8,12},{12,16},{16,20},{20,24},{24,28},{1,5},{5,9},{9,... | collective-permute-start | bytes 829448 | tf_op jit(solution)/shard_map/ppermute | solution.py:37
  130.0 1.3 collective-permute-start.16
  131.3 2.4 %tracer_edges.1 = (f32[8,2,8,88]{3,2,1,0:T(8,128)}, f32[8,2,8,88]{3,2,1,0:T(8,128)}) custom-call(f32[8,2,88,1440]{3,2,1,0:T(8,128)} %refs_0_.7, f32[8,2,88,1440]{3,2,1,0:T(8,128)} %refs_0_.7), custom_call_target="tpu_custom_call" | custom-call | tf_op jit(solution)/shard_map/tracer_edges/pallas_call | solution.py:290
  133.7 1.2 collective-permute-start.13
  135.3 0.3 copy-done.7
  135.7 0.4 multiply_subtract_fusion.2
  136.1 1.3 maximum_maximum_fusion.2.refs_3_
  137.4 11.4 %substep.5 = (f32[2,96,1536]{2,1,0:T(8,128)}, f32[2,96,1536]{2,1,0:T(8,128)}, f32[2,96,1536]{2,1,0:T(8,128)}, f32[2,96,1536]{2,1,0:T(8,128)}, f32[2,88,1440]{2,1...) custom-call(f32[2,96,1536]{2,1,0:T(8,128)} %get-tuple-element.49.refs_0_, ...), custom_call_target="tpu_custom_call" | custom-call | tf_op jit(solution)/shard_map/substep/pallas_call | solution.py:420
  148.9 0.6 copy-done.2
  149.4 41.9 %tracers.1 = f32[8,2,88,1440]{3,2,1,0:T(8,128)} custom-call(f32[8,2,88,1440]{3,2,1,0:T(8,128)} %refs_0_.7, f32[8,2,8,88]{3,2,1,0:T(8,128)} %copy-done.2, f32[8,2,8,88]{3,2,1,0:T(8,128)} %copy-done.3, f32[8,2,3,1440]{3,2,1,0:T(4,128)} %collective-permute-done.15.refs_3_, f32[8,2,3,1440]{3,2,1,0:T(4,128)} %collective-permute-done.16.refs_4_, ...), custom_call_target="tpu_custom_call" | custom-call | tf_op jit(solution)/shard_map/tracers/pallas_call | solution.py:442
  (64 shorter events, 2.7 us)
Async XLA Ops:
  2.7 8.7 %collective-permute-start.1 = (f32[3,2,3,1440]{3,2,1,0:T(4,128)S(1)}, f32[3,2,3,1440]{3,2,1,0:T(4,128)S(1)}, u32[]{:S(2)}, u32[]{:S(2)}) collective-permute-start(f32[3,2,3,1440]{3,2,1,0:T(4,128)S(1)} %pad_maximum_fusion.7), channel_id=1, source_target_pairs={{4,0},{8,4},{12,8},{16,12},{20,16},{24,20},{28,24},{5,1},{9,5},{13... | collective-permute-start | bytes 311048 | tf_op jit(solution)/shard_map/ppermute | solution.py:37
  4.1 10.7 %collective-permute-start = (f32[3,2,3,1440]{3,2,1,0:T(4,128)S(1)}, f32[3,2,3,1440]{3,2,1,0:T(4,128)S(1)}, u32[]{:S(2)}, u32[]{:S(2)}) collective-permute-start(f32[3,2,3,1440]{3,2,1,0:T(4,128)S(1)} %pad_maximum_fusion.6), channel_id=1, source_target_pairs={{0,4},{4,8},{8,12},{12,16},{16,20},{20,24},{24,28},{1,5},{5,9},{9,... | collective-permute-start | bytes 311048 | tf_op jit(solution)/shard_map/ppermute | solution.py:37
  11.4 3.3 %copy-start = (f32[3,2,3,1440]{3,2,1,0:T(4,128)}, f32[3,2,3,1440]{3,2,1,0:T(4,128)S(1)}, u32[]{:S(2)}) copy-start(f32[3,2,3,1440]{3,2,1,0:T(4,128)S(1)} %collective-permute-done.1.refs_8_.refs_9_.refs_4_) | copy-start | bytes 311044
  14.7 0.7 copy-start.1
  17.4 2.9 %collective-permute-start.2 = (f32[3,2,8,96]{3,2,1,0:T(8,128)}, f32[3,2,8,96]{3,2,1,0:T(8,128)S(1)}, u32[]{:S(2)}, u32[]{:S(2)}) collective-permute-start(f32[3,2,8,96]{3,2,1,0:T(8,128)} %get-tuple-element.35), channel_id=1, source_target_pairs={{0,3},{1,0},{2,1},{3,2},{4,7},{5,4},{6,5},{7,6},{8,11},{9,8},{10,9... | collective-permute-start | bytes 55304 | tf_op jit(solution)/shard_map/ppermute | solution.py:37
  18.5 3.5 %collective-permute-start.3 = (f32[3,2,8,96]{3,2,1,0:T(8,128)}, f32[3,2,8,96]{3,2,1,0:T(8,128)S(1)}, u32[]{:S(2)}, u32[]{:S(2)}) collective-permute-start(f32[3,2,8,96]{3,2,1,0:T(8,128)} %get-tuple-element.36), channel_id=1, source_target_pairs={{0,1},{1,2},{2,3},{3,0},{4,5},{5,6},{6,7},{7,4},{8,9},{9,10},{10,1... | collective-permute-start | bytes 55304 | tf_op jit(solution)/shard_map/ppermute | solution.py:37
  20.3 1.7 copy-start.4
  22.0 0.6 copy-start.5
  33.8 2.4 %collective-permute-start.4 = (f32[192,1024]{1,0:T(8,128)S(1)}, f32[192,1024]{1,0:T(8,128)S(1)}, u32[]{:S(2)}, u32[]{:S(2)}) collective-permute-start(f32[192,1024]{1,0:T(8,128)S(1)} %select_bitcast_fusion.2), channel_id=1, source_target_pairs={{0,1},{1,0},{2,3},{3,2},{4,5},{5,4},{6,7},{7,6},{8,9},{9,8},{10,11... | collective-permute-start | bytes 2359304 | tf_op jit(solution)/shard_map/ppermute | solution.py:265
  36.4 19.9 %copy-start.8 = (s32[176]{0:T(256)S(1)}, s32[176]{0:T(256)}, u32[]{:S(2)}) copy-start(s32[176]{0:T(256)} %param.13) | copy-start | bytes 2116
  36.4 19.6 %collective-permute-start.5 = (f32[192,1024]{1,0:T(8,128)S(1)}, f32[192,1024]{1,0:T(8,128)S(1)}, u32[]{:S(2)}, u32[]{:S(2)}) collective-permute-start(f32[192,1024]{1,0:T(8,128)S(1)} %bitcast_add_fusion), channel_id=1, source_target_pairs={{0,2},{1,3},{2,0},{3,1},{4,6},{5,7},{6,4},{7,5},{8,10},{9,11},{10,... | collective-permute-start | bytes 2359304 | tf_op jit(solution)/shard_map/ppermute | solution.py:266
  56.1 2.4 %collective-permute-start.6 = (f32[192,1024]{1,0:T(8,128)S(1)}, f32[192,1024]{1,0:T(8,128)S(1)}, u32[]{:S(2)}, u32[]{:S(2)}) collective-permute-start(f32[192,1024]{1,0:T(8,128)S(1)} %add.181), channel_id=1, source_target_pairs={{0,1},{1,0},{2,3},{3,2},{4,5},{5,4},{6,7},{7,6},{8,9},{9,8},{10,11... | collective-permute-start | bytes 2359304 | tf_op jit(solution)/shard_map/ppermute | solution.py:267
  76.3 1.8 collective-permute-start.7
  78.2 11.2 %collective-permute-start.8 = (f32[96,1024]{1,0:T(8,128)S(1)}, f32[96,1024]{1,0:T(8,128)S(1)}, u32[]{:S(2)}, u32[]{:S(2)}) collective-permute-start(f32[96,1024]{1,0:T(8,128)S(1)} %bitcast_add_fusion.2), channel_id=1, source_target_pairs={{0,2},{1,3},{2,0},{3,1},{4,6},{5,7},{6,4},{7,5},{8,10},{9,11},{10,... | collective-permute-start | bytes 1179656 | tf_op jit(solution)/shard_map/ppermute | solution.py:266
  89.5 1.8 collective-permute-start.9
  89.6 2.1 %copy-start.6 = (f32[96]{0:T(128)}, f32[96]{0:T(128)S(1)}, u32[]{:S(2)}) copy-start(f32[96]{0:T(128)S(1)} %and_convert_fusion) | copy-start | bytes 1156
  110.2 1.8 collective-permute-start.10
  112.0 11.2 %collective-permute-start.11 = (f32[96,1024]{1,0:T(8,128)S(1)}, f32[96,1024]{1,0:T(8,128)S(1)}, u32[]{:S(2)}, u32[]{:S(2)}) collective-permute-start(f32[96,1024]{1,0:T(8,128)S(1)} %bitcast_add_fusion.1), channel_id=1, source_target_pairs={{0,2},{1,3},{2,0},{3,1},{4,6},{5,7},{6,4},{7,5},{8,10},{9,11},{10,... | collective-permute-start | bytes 1179656 | tf_op jit(solution)/shard_map/ppermute | solution.py:266
  123.3 11.6 %collective-permute-start.12 = (f32[96,1024]{1,0:T(8,128)S(1)}, f32[96,1024]{1,0:T(8,128)S(1)}, u32[]{:S(2)}, u32[]{:S(2)}) collective-permute-start(f32[96,1024]{1,0:T(8,128)S(1)} %add.196), channel_id=1, source_target_pairs={{0,1},{1,0},{2,3},{3,2},{4,5},{5,4},{6,7},{7,6},{8,9},{9,8},{10,11... | collective-permute-start | bytes 1179656 | tf_op jit(solution)/shard_map/ppermute | solution.py:267
  124.9 23.9 %collective-permute-start.15 = (f32[8,2,3,1440]{3,2,1,0:T(4,128)S(1)}, f32[8,2,3,1440]{3,2,1,0:T(4,128)}, u32[]{:S(2)}, u32[]{:S(2)}) collective-permute-start(f32[8,2,3,1440]{3,2,1,0:T(4,128)S(1)} %get-tuple-element.73), channel_id=1, source_target_pairs={{0,4},{4,8},{8,12},{12,16},{16,20},{20,24},{24,28},{1,5},{5,9},{9,... | collective-permute-start | bytes 829448 | tf_op jit(solution)/shard_map/ppermute | solution.py:37
  130.0 18.8 %collective-permute-start.16 = (f32[8,2,3,1440]{3,2,1,0:T(4,128)S(1)}, f32[8,2,3,1440]{3,2,1,0:T(4,128)}, u32[]{:S(2)}, u32[]{:S(2)}) collective-permute-start(f32[8,2,3,1440]{3,2,1,0:T(4,128)S(1)} %get-tuple-element.72), channel_id=1, source_target_pairs={{4,0},{8,4},{12,8},{16,12},{20,16},{24,20},{28,24},{5,1},{9,5},{13... | collective-permute-start | bytes 829448 | tf_op jit(solution)/shard_map/ppermute | solution.py:37
  133.7 15.1 %collective-permute-start.13 = (f32[8,2,8,88]{3,2,1,0:T(8,128)}, f32[8,2,8,88]{3,2,1,0:T(8,128)S(1)}, u32[]{:S(2)}, u32[]{:S(2)}) collective-permute-start(f32[8,2,8,88]{3,2,1,0:T(8,128)} %get-tuple-element.60), channel_id=1, source_target_pairs={{0,3},{1,0},{2,1},{3,2},{4,7},{5,4},{6,5},{7,6},{8,11},{9,8},{10,9... | collective-permute-start | bytes 135176 | tf_op jit(solution)/shard_map/ppermute | solution.py:37
  134.9 13.9 %collective-permute-start.14 = (f32[8,2,8,88]{3,2,1,0:T(8,128)}, f32[8,2,8,88]{3,2,1,0:T(8,128)S(1)}, u32[]{:S(2)}, u32[]{:S(2)}) collective-permute-start(f32[8,2,8,88]{3,2,1,0:T(8,128)} %get-tuple-element.61), channel_id=1, source_target_pairs={{0,1},{1,2},{2,3},{3,0},{4,5},{5,6},{6,7},{7,4},{8,9},{9,10},{10,1... | collective-permute-start | bytes 135176 | tf_op jit(solution)/shard_map/ppermute | solution.py:37
  135.0 0.7 copy-start.7
  148.8 0.6 copy-start.2
  148.8 0.6 copy-start.3

commit v2 on v1

v2 whole, which is shorter than its diff:
```python
import math

import numpy as np
import jax
import jax.numpy as jnp
from jax import lax
from jax.experimental import pallas as pl
from jax.experimental.pallas import tpu as pltpu
from jax.sharding import PartitionSpec as P

NLON = 5760
KMAX = 512
SUBSTEPS = 3

LAT_EDGE = 85.0 * math.pi / 180.0
PRESSURE_PUSH = 0.08
DIVERGE_RATE = 0.08
COURANT_RATE = 0.3

HALO = 3
SOUTH_PAD = 4
SIDE = 8
VMEM_LIMIT = 56 * 1024 * 1024


def center_cos(global_rows, total_rows):
    return jnp.cos(((2 * global_rows + 1).astype(jnp.float32) / total_rows - 1.0) * LAT_EDGE)


def face_cos(global_rows, total_rows):
    return jnp.cos(((2 * global_rows + 2).astype(jnp.float32) / total_rows - 1.0) * LAT_EDGE)


def shifted(array, axis, by, wrap):
    count = lax.axis_size(axis)
    pairs = [(i, (i + by) % count) for i in range(count) if wrap or 0 <= i + by < count]
    return lax.ppermute(array, axis, pairs)


def split_bf16(values):
    high = values.astype(jnp.bfloat16)
    low = (values - high.astype(jnp.float32)).astype(jnp.bfloat16)
    return high, low


def basis_table(width, lanes):
    lane = np.arange(lanes)
    column = np.where(lane < (width + lanes) // 2, lane, lane - lanes)
    phase = (column[:, None] * np.arange(KMAX)[None, :]) % NLON
    angle = phase * (2.0 * math.pi / NLON)
    table = np.concatenate([np.cos(angle), np.sin(angle)], axis=1).astype(np.float32)
    high = table.astype(jnp.bfloat16)
    low = (table - high.astype(np.float32)).astype(jnp.bfloat16)
    return jnp.asarray(high), jnp.asarray(low)


def shift_tables(own_rows):
    faces, cells = own_rows + 8, own_rows + 24
    table = np.zeros((5, faces, cells), np.float32)
    for at in range(own_rows + 1):
        for which, move in enumerate((0, -1, 1)):
            centre = 7 + at + move
            table[which, at, centre - 1 : centre + 3] = (-1, 7, 7, -1)
        table[3, at, 7 + at] = 1
        table[4, at, 8 + at] = 1
    table = table.reshape(5 * faces, cells)
    change = np.zeros((own_rows, faces), np.float32)
    for at in range(own_rows):
        change[at, at : at + 2] = (-1, 1)
    double = lambda x: jnp.asarray(np.concatenate([x, x], axis=1).astype(jnp.bfloat16))
    return double(table), double(change)


def dot3(values, high_ref, low_ref, transposed):
    high, low = split_bf16(values)
    sides = (((1,), (1 if transposed else 0,)), ((), ()))

    def dot(x, ref):
        return lax.dot_general(x, ref[...], sides, preferred_element_type=jnp.float32)

    return dot(high, high_ref) + dot(low, high_ref) + dot(high, low_ref)


def two_parts(values):
    return jnp.concatenate(split_bf16(values), axis=0)


def turned(sums, turn_cos, turn_sin):
    a, b = sums[:, :KMAX], sums[:, KMAX:]
    return jnp.concatenate([a * turn_cos - b * turn_sin, a * turn_sin + b * turn_cos], axis=1)


def forward(values, width, rows_ref, waves_ref, bh_ref, bl_ref, kept_out, sent_out):
    lane = lax.broadcasted_iota(jnp.int32, values.shape, 1)
    sums = dot3(jnp.where(lane < width, values, 0.0), bh_ref, bl_ref, False)
    sums = turned(sums, waves_ref[0:1, :], waves_ref[1:2, :])
    half = sums.shape[0] // 2
    even = rows_ref[0:half, 5:6] > 0.0
    kept_out[...] = jnp.where(even, sums[:half], sums[half:])
    sent_out[...] = jnp.where(even, sums[half:], sums[:half])


def ahead(values, axis):
    return pltpu.roll(values, values.shape[axis] - 1, axis)


def behind(values, axis):
    return pltpu.roll(values, 1, axis)


def push_winds(p, u, v, rows):
    u = u - rows[:, 0:1] * (ahead(p, 1) - p)
    v = (v - PRESSURE_PUSH * (ahead(p, 0) - p)) * rows[:, 1:2]
    return u, v


def edge_columns(first, last, width):
    end = width % 128
    return first.T[:SIDE], last.T[end - SIDE : end]


def side_lanes(east, west, width):
    end = width % 128
    rows = east.shape[1]
    fill = jnp.zeros((end, rows), jnp.float32)
    gap = jnp.zeros((128 - end - 2 * SIDE, rows), jnp.float32)
    return jnp.concatenate([fill, east, gap, west], axis=0).T


def tracer_edges(width, first_ref, last_ref, head_out, tail_out):
    for t in range(first_ref.shape[0]):
        for l in range(first_ref.shape[1]):
            head, tail = edge_columns(first_ref[t, l], last_ref[t, l], width)
            head_out[t, l] = head
            tail_out[t, l] = tail


def field_edges(width, *refs):
    fields, (south, north), (head_out, tail_out, block) = refs[:6], (refs[6:8], refs[8:10]), refs[10:]
    levels, own_rows = fields[0].shape[:2]
    for f in range(3):
        for l in range(levels):
            sides = []
            for end in range(2):
                block[...] = jnp.zeros_like(block)
                block[SOUTH_PAD - HALO : SOUTH_PAD] = south[end][f, l]
                block[SOUTH_PAD : SOUTH_PAD + own_rows] = fields[2 * f + end][l]
                block[SOUTH_PAD + own_rows : SOUTH_PAD + own_rows + HALO] = north[end][f, l]
                sides.append(block[...])
            head, tail = edge_columns(sides[0], sides[1], width)
            head_out[f, l] = head
            tail_out[f, l] = tail


def substeps_kernel(
    p_ref, u_ref, v_ref, south_ref, north_ref, east_ref, west_ref, rows_ref, waves_ref, bh_ref,
    bl_ref, p_out, u_out, v_out, fx_out, fy_out, ua_out, va_out, wide, spectrum, big, small,
    send_sem, recv_sem
):
    levels, own_rows, width = p_ref.shape
    whole = width // 128 * 128
    own = slice(SOUTH_PAD, SOUTH_PAD + own_rows)
    count = rows_ref.shape[0]
    me = lax.axis_index("lon")
    sibling = me + 1 - 2 * lax.rem(me, 2)
    across = lax.rem(me + 2, 4)
    mesh_id = pl.DeviceIdType.MESH

    barrier = pltpu.get_barrier_semaphore()
    for partner in (sibling, across):
        pl.semaphore_signal(barrier, inc=1, device_id={"lon": partner}, device_id_type=mesh_id)

    KEPT, SENT, FROM_CORE, FROM_CHIP, LAST_HALF, HALF, TOTAL = range(7)

    def slot(s, l, role):
        return big.at[l, role] if s == 0 else small.at[s - 1, l, role]

    def copy(s, l, stage):
        source, target, partner = (
            (SENT, FROM_CORE, sibling), (HALF, FROM_CHIP, across), (TOTAL, LAST_HALF, sibling)
        )[stage]
        at = (s * levels + l) * 3 + stage
        return pltpu.make_async_remote_copy(
            src_ref=slot(s, l, source),
            dst_ref=slot(s, l, target),
            send_sem=send_sem.at[at],
            recv_sem=recv_sem.at[at],
            device_id={"lon": partner},
            device_id_type=mesh_id,
        )

    def to_chip(s, l):
        copy(s, l, 0).wait()
        slot(s, l, HALF)[...] = slot(s, l, KEPT)[...] + slot(s, l, FROM_CORE)[...]
        copy(s, l, 1).start()

    def to_core(s, l):
        copy(s, l, 1).wait()
        slot(s, l, TOTAL)[...] = slot(s, l, HALF)[...] + slot(s, l, FROM_CHIP)[...]
        copy(s, l, 2).start()

    def send_forward(s, l, values):
        forward(
            values, width, rows_ref, waves_ref, bh_ref, bl_ref, slot(s, l, KEPT), slot(s, l, SENT)
        )
        copy(s, l, 0).start()

    def push(l):
        u, v = push_winds(wide[0, l], wide[1, l], wide[2, l], rows_ref[...])
        wide[1, l] = u
        wide[2, l] = v
        return u, v

    def summed(s, l):
        copy(s, l, 2).wait()
        half, other = slot(s, l, TOTAL)[...], slot(s, l, LAST_HALF)[...]
        even = rows_ref[0 : half.shape[0], 5:6] > 0.0
        total = jnp.concatenate(
            [jnp.where(even, half, other), jnp.where(even, other, half)], axis=0
        )
        return turned(total, waves_ref[0:1, :], -waves_ref[1:2, :])

    def coefficients(s, l):
        total = summed(s, l)
        rows = rows_ref[...]
        wave = lax.broadcasted_iota(jnp.int32, (count, KMAX), 1).astype(jnp.float32)
        weight = jnp.where(wave < rows[:, 6:7], waves_ref[4:5, :], 0.0)
        weight = jnp.concatenate([weight, weight], axis=1)
        if s == 0:
            spectrum[l] = total * jnp.concatenate([weight, weight], axis=0)
            return
        pa, pb = total[:, :KMAX], total[:, KMAX:]
        less, sine = waves_ref[2:3, :], waves_ref[3:4, :]
        east = jnp.concatenate([less * pa + sine * pb, less * pb - sine * pa], axis=1)
        spectrum[l, :count] = spectrum[l, :count] - rows[:, 0:1] * weight * east
        spectrum[l, count:] = (
            spectrum[l, count:] - PRESSURE_PUSH * weight * (ahead(total, 0) - total)
        ) * rows[:, 1:2]

    def step(s, l):
        coefficients(s, l)
        rows = rows_ref[...]
        smooth = dot3(spectrum[l], bh_ref, bl_ref, True)
        polar = rows[:, 3:4] > 0.0
        p = wide[0, l]
        u = jnp.where(polar, smooth[:count], wide[1, l])
        v = jnp.where(polar, smooth[count:], wide[2, l])
        flux_x = 0.5 * (p + ahead(p, 1)) * u
        flux_y = (p + ahead(p, 0)) * v * rows[:, 2:3]
        p = p - rows[:, 0:1] * ((flux_x - behind(flux_x, 1)) + (flux_y - behind(flux_y, 0)))
        for out, term in ((fx_out, flux_x), (fy_out, flux_y), (ua_out, u), (va_out, v)):
            out[l] = term if s == 0 else out[l] + term
        if s == SUBSTEPS - 1:
            p_out[l] = p[own, :width]
            u_out[l] = u[own, :width]
            v_out[l] = v[own, :width]
        else:
            wide[0, l] = p
            wide[1, l] = u
            wide[2, l] = v

    for l in range(levels):
        for at, ref in enumerate((p_ref, u_ref, v_ref)):
            wide[at, l] = jnp.zeros((count, wide.shape[3]), jnp.float32)
            wide[at, l, SOUTH_PAD - HALO : SOUTH_PAD, :width] = south_ref[at, l]
            wide[at, l, own, :width] = ref[l]
            wide[at, l, SOUTH_PAD + own_rows : SOUTH_PAD + own_rows + HALO, :width] = north_ref[at, l]
            wide[at, l, :, whole:] = wide[at, l, :, whole:] + side_lanes(
                east_ref[at, l], west_ref[at, l], width
            )
    pl.semaphore_wait(barrier, 2)

    for l in range(levels):
        both = jnp.concatenate(push(l), axis=0)
        if l > 0:
            to_chip(0, l - 1)
        send_forward(0, l, both)
    to_chip(0, levels - 1)
    for s in range(SUBSTEPS):
        more = s < SUBSTEPS - 1
        to_core(s, 0)
        for l in range(levels):
            step(s, l)
            if l + 1 < levels:
                to_core(s, l + 1)
            if more:
                if l > 0:
                    to_chip(s + 1, l - 1)
                send_forward(s + 1, l, wide[0, l])
                push(l)
        if more:
            to_chip(s + 1, levels - 1)


def tracer_kernel(
    own_rows, width, q_ref, east_ref, west_ref, south_ref, north_ref, thick_ref, fx_ref, fy_ref, ua_ref, va_ref, rows_ref,
    shift_ref, change_ref, out_ref, ext, cx, xa, xe, xq, cy, ya, ye, yq, row_k
):
    lanes = ext.shape[1]
    whole = width // 128 * 128

    @pl.when(pl.program_id(1) == 0)
    def _():
        ext[...] = jnp.zeros_like(ext)
        for ref in (cy, ya, ye, yq):
            ref[...] = jnp.zeros_like(ref)

        def coefficients(mass, courant):
            size = jnp.abs(courant)
            slope = mass * size * 0.5
            curve = slope * (1.0 - size * (2.0 / 3.0))
            near = (mass - slope - 3.0 * curve) * (1.0 / 12.0)
            far = (slope - 3.0 * curve) * (1.0 / 12.0)
            return near, far, 6.0 * curve

        own = pl.ds(SOUTH_PAD, own_rows)
        k = rows_ref[own, 0:1]
        c = jnp.clip(rows_ref[own, 4:5] * ua_ref[0, own, :], -1.0, 1.0)
        cx[...] = c
        near, far, cell = coefficients(fx_ref[0, own, :] * k, c)
        xa[...] = near
        xe[...] = far
        xq[...] = cell
        faces = pl.ds(SOUTH_PAD - 1, own_rows + 1)
        at = pl.ds(0, own_rows + 1)
        c = jnp.clip(COURANT_RATE * va_ref[0, faces, :], -1.0, 1.0)
        cy[at, :] = c
        near, far, cell = coefficients(fy_ref[0, faces, :], c)
        ya[at, :] = near
        ye[at, :] = far
        yq[at, :] = cell
        row_k[...] = jnp.broadcast_to(k, row_k.shape)

    ext[8 - HALO : 8, 0:width] = south_ref[0, 0]
    ext[8 + own_rows : 8 + own_rows + HALO, 0:width] = north_ref[0, 0]
    ext[8 : 8 + own_rows, 0:width] = q_ref[0, 0]
    tail = ext[8 : 8 + own_rows, whole:lanes]
    sides = side_lanes(east_ref[0, 0], west_ref[0, 0], width)
    lane = lax.broadcasted_iota(jnp.int32, tail.shape, 1)
    ext[8 : 8 + own_rows, whole:lanes] = jnp.where(lane < width - whole, tail, sides)

    for at in range(0, own_rows, 8):
        here = slice(at, at + 8)
        q = ext[8 + at : 16 + at, :]
        q_next = ahead(q, 1)
        a = 7.0 * (q + q_next) - (behind(q, 1) + pltpu.roll(q, lanes - 2, 1))
        positive = cx[here, :] > 0.0
        e = jnp.where(positive, behind(a, 1), ahead(a, 1))
        cell = jnp.where(positive, q, q_next)
        f = xa[here, :] * a + xe[here, :] * e + xq[here, :] * cell
        f = f - behind(f, 1)
        out_ref[0, 0, here, :] = q[:, :width] * thick_ref[0, here, :] - f[:, :width]

    faces = own_rows + 8
    for at in range(0, lanes, 256):
        here = slice(at, at + 256)
        parts = two_parts(ext[:, here])
        moved = jnp.dot(shift_ref[...], parts, preferred_element_type=jnp.float32)
        edge, edge_before, edge_after, cell, cell_after = [
            moved[n * faces : (n + 1) * faces] for n in range(5)
        ]
        positive = cy[:, here] > 0.0
        flux = (
            ya[:, here] * edge
            + ye[:, here] * jnp.where(positive, edge_before, edge_after)
            + yq[:, here] * jnp.where(positive, cell, cell_after)
        )
        change = jnp.dot(change_ref[...], two_parts(flux), preferred_element_type=jnp.float32)
        size = min(256, width - at)
        there = slice(at, at + size)
        out_ref[0, 0, :, there] = out_ref[0, 0, :, there] - (row_k[...] * change)[:, :size]


def local(thickness, zonal_wind, merid_wind, tracers, cutoffs):
    levels, own_rows, width = thickness.shape
    tracer_count = tracers.shape[0]
    total_rows = own_rows * lax.axis_size("lat")
    lanes = (width // 128 + 1) * 128
    ext_rows = own_rows + 8
    f32 = jnp.float32

    whole = width // 128 * 128
    q_south = shifted(tracers[:, :, -HALO:], "lat", 1, False)
    q_north = shifted(tracers[:, :, :HALO], "lat", -1, False)
    south = shifted(
        jnp.stack([x[:, -HALO:] for x in (thickness, zonal_wind, merid_wind)]), "lat", 1, False
    )
    north = shifted(
        jnp.stack([x[:, :HALO] for x in (thickness, zonal_wind, merid_wind)]), "lat", -1, False
    )
    q_block = (tracer_count, levels, own_rows, 128)
    q_side = jax.ShapeDtypeStruct((tracer_count, levels, SIDE, own_rows), f32)
    q_head, q_tail = pl.pallas_call(
        lambda *refs: tracer_edges(width, *refs),
        grid=(1,),
        in_specs=[
            pl.BlockSpec(q_block, lambda i: (0, 0, 0, 0)),
            pl.BlockSpec(q_block, lambda i: (0, 0, 0, whole // 128)),
        ],
        out_specs=[pl.BlockSpec(q_side.shape, lambda i: (0, 0, 0, 0))] * 2,
        out_shape=[q_side] * 2,
        name="tracer_edges",
    )(tracers, tracers)
    q_west = shifted(q_tail, "lon", 1, True)
    q_east = shifted(q_head, "lon", -1, True)

    side = jax.ShapeDtypeStruct((3, levels, SIDE, ext_rows), f32)
    own_block, cap_block = (levels, own_rows, 128), (3, levels, HALO, 128)
    ends = [0, whole // 128]
    head, tail = pl.pallas_call(
        lambda *refs: field_edges(width, *refs),
        grid=(1,),
        in_specs=[pl.BlockSpec(own_block, lambda i, e=e: (0, 0, e)) for _ in range(3) for e in ends]
        + [pl.BlockSpec(cap_block, lambda i, e=e: (0, 0, 0, e)) for _ in range(2) for e in ends],
        out_specs=[pl.BlockSpec(side.shape, lambda i: (0, 0, 0, 0))] * 2,
        out_shape=[side] * 2,
        scratch_shapes=[pltpu.VMEM((ext_rows, 128), f32)],
        name="field_edges",
    )(
        thickness, thickness, zonal_wind, zonal_wind, merid_wind, merid_wind,
        south, south, north, north,
    )
    west = shifted(tail, "lon", 1, True)
    east = shifted(head, "lon", -1, True)

    global_rows = (
        lax.axis_index("lat") * own_rows - SOUTH_PAD + jnp.arange(ext_rows, dtype=jnp.int32)
    )
    cos_center = center_cos(global_rows, total_rows)
    wall = ((global_rows >= 0) & (global_rows < total_rows - 1)).astype(f32)
    polar = total_rows // 8
    is_polar = ((global_rows >= 0) & (global_rows < polar)) | (
        (global_rows >= total_rows - polar) & (global_rows < total_rows)
    )
    rate = DIVERGE_RATE / cos_center
    slot = jnp.where(global_rows < polar, global_rows, global_rows - total_rows + 2 * polar)
    matches = slot[:, None] == jnp.arange(2 * polar, dtype=jnp.int32)[None, :]
    row_cut = jnp.sum(jnp.where(matches, cutoffs[None, :], 0), axis=1)
    even = jnp.broadcast_to(lax.axis_index("lon") % 2 == 0, (ext_rows,))
    columns = [
        rate, wall, 0.5 * face_cos(global_rows, total_rows) * wall, is_polar.astype(f32),
        COURANT_RATE / cos_center, even.astype(f32), row_cut.astype(f32),
    ]
    rows = jnp.pad(jnp.stack(columns, axis=1), ((0, 0), (0, 128 - len(columns))))

    waves = jnp.arange(KMAX, dtype=jnp.int32)
    step_angle = 2.0 * math.pi / NLON
    phase = (lax.axis_index("lon") * width * waves) % NLON
    turn = phase.astype(f32) * step_angle
    wave_angle = waves.astype(f32) * step_angle
    by_wave = [
        jnp.cos(turn), jnp.sin(turn), -2.0 * jnp.sin(0.5 * wave_angle) ** 2, jnp.sin(wave_angle),
        jnp.where(waves == 0, 1.0, 2.0).astype(f32) / NLON,
    ]
    wave_rows = jnp.pad(jnp.stack(by_wave), ((0, 8 - len(by_wave)), (0, 0)))

    bh, bl = basis_table(width, lanes)
    shift, change = shift_tables(own_rows)

    def f32_shape(*shape):
        return jax.ShapeDtypeStruct(shape, f32)

    in_vmem = pl.BlockSpec(memory_space=pltpu.VMEM)
    ins = [
        thickness, zonal_wind, merid_wind, south, north, east, west, rows, wave_rows, bh, bl
    ]
    wide_shape = f32_shape(levels, ext_rows, lanes)
    copies = 3 * SUBSTEPS * levels
    p, u, v, *sums = pl.pallas_call(
        substeps_kernel,
        in_specs=[in_vmem] * len(ins),
        out_specs=[in_vmem] * 7,
        out_shape=[f32_shape(*thickness.shape)] * 3 + [wide_shape] * 4,
        scratch_shapes=[
            pltpu.VMEM((3, levels, ext_rows, lanes), f32),
            pltpu.VMEM((levels, 2 * ext_rows, 2 * KMAX), f32),
            pltpu.VMEM((levels, 7, ext_rows, 2 * KMAX), f32),
            pltpu.VMEM((SUBSTEPS - 1, levels, 7, ext_rows // 2, 2 * KMAX), f32),
            pltpu.SemaphoreType.DMA((copies,)),
            pltpu.SemaphoreType.DMA((copies,)),
        ],
        compiler_params=pltpu.CompilerParams(
            collective_id=0, has_side_effects=True, vmem_limit_bytes=VMEM_LIMIT
        ),
        cost_estimate=pl.CostEstimate(
            flops=30_000_000_000, bytes_accessed=100_000_000, transcendentals=0
        ),
        name="substeps",
    )(*ins)

    def by_tracer(*shape):
        return pl.BlockSpec((1, 1) + shape, lambda l, t: (t, l, 0, 0))

    def by_level(*shape):
        return pl.BlockSpec((1,) + shape, lambda l, t: (l, 0, 0))

    def table(array):
        return pl.BlockSpec(array.shape, lambda l, t: (0, 0))

    tracer_mass = pl.pallas_call(
        lambda *refs: tracer_kernel(own_rows, width, *refs),
        grid=(levels, tracer_count),
        in_specs=[by_tracer(own_rows, width)]
        + [by_tracer(SIDE, own_rows)] * 2
        + [by_tracer(HALO, width)] * 2
        + [by_level(own_rows, width)]
        + [by_level(ext_rows, lanes)] * 4
        + [table(rows), table(shift), table(change)],
        out_specs=by_tracer(own_rows, width),
        out_shape=f32_shape(*tracers.shape),
        scratch_shapes=[pltpu.VMEM((own_rows + 24, lanes), f32)]
        + [pltpu.VMEM((own_rows, lanes), f32)] * 4
        + [pltpu.VMEM((own_rows + 8, lanes), f32)] * 4
        + [pltpu.VMEM((own_rows, 256), f32)],
        compiler_params=pltpu.CompilerParams(
            dimension_semantics=("arbitrary", "arbitrary"), vmem_limit_bytes=VMEM_LIMIT
        ),
        name="tracers",
    )(tracers, q_east, q_west, q_south, q_north, thickness, *sums, rows, shift, change)
    return (p, u, v, tracer_mass)


def solution(mesh):
    return jax.shard_map(
        local,
        mesh=mesh,
        in_specs=(
            P(None, "lat", "lon"),
            P(None, "lat", "lon"),
            P(None, "lat", "lon"),
            P(None, None, "lat", "lon"),
            P(),
        ),
        out_specs=(
            P(None, "lat", "lon"),
            P(None, "lat", "lon"),
            P(None, "lat", "lon"),
            P(None, None, "lat", "lon"),
        ),
        check_vma=False,
    )
```

time: 192 us -> 147 us (0.77)
  waiting for transfers between devices: 54.9 us -> 3.75 us
  Pallas kernels: 97.3 us -> 117 us
  other arithmetic: 11.2 us -> 0.55 us
  starting transfers between devices: 20.1 us -> 13.7 us
  local copies, waits for them, and re-layouts: 6.8 us -> 11.3 us
    ppermute x9 -> x0, waiting for transfers between devices: 47.2 us -> none  [the longest x3 38.1 us: circle_sums(): half = half + lax.ppermute(half, 'lon', across)]
    pallas_call x4 -> x1, Pallas kernels: 51 us -> 71.1 us  [local(): pl.pallas_call(substeps_kernel, in_specs=[in_vmem] * len(ins), out_specs=...]
    sub x7 -> x0, other arithmetic: 5.24 us -> none  [the longest x3 4.06 us: summed(): a * turn_cos - b * turn_sin]
    ppermute x9 -> x0, starting transfers between devices: 4.62 us -> none  [the longest x3 3.94 us: circle_sums(): half = half + lax.ppermute(half, 'lon', across)]
    unnamed x18 -> x27, local copies, waits for them, and re-layouts: 2.23 us -> 6.36 us
    ppermute x8, waiting for transfers between devices: 7.66 us -> 3.75 us  [shifted(): return lax.ppermute(array, axis, pairs)]
    concatenate x3 -> x0, other arithmetic: 3.84 us -> none  [local(): jnp.concatenate([jnp.concatenate([ua, ub], axis=-1), jnp.concatenate([va,...]
  transfers between devices with their start and end apart: 17 -> 8, of which waited for: 12 -> 2; matrix products, arithmetic and copies ran while one was open for 3% -> 4% of each run, Pallas kernels for 7% -> 50%
where the time goes in v2:
time: 147 us
  Pallas kernels  117 us (80%)
  starting transfers between devices  13.7 us (9%)
  local copies, waits for them, and re-layouts  11.3 us (8%)
  waiting for transfers between devices  3.75 us (3%)
    pallas_call x1, Pallas kernels, local(): pl.pallas_call(substeps_kernel, in_specs=[in_vmem] * len(ins), out_specs=...  71.1 us
    pallas_call x1, Pallas kernels, local(): pl.pallas_call(lambda *refs: tracer_kernel(own_rows, width, *refs), grid=...  41.2 us
    ppermute x8, starting transfers between devices, shifted(): return lax.ppermute(array, axis, pairs)  13.7 us
    unnamed x27, local copies, waits for them, and re-layouts  6.36 us
    ppermute x8, waiting for transfers between devices, shifted(): return lax.ppermute(array, axis, pairs)  3.75 us
  transfers between devices with their start and end apart: 8, of which 2 were waited for; matrix products, arithmetic and copies ran while one was open for 4% of the time, Pallas kernels for 50%

profile of v2, /device:TPU:0, one launch (start us, length us, event | category | flops | bytes accessed | tf_op | source)
XLA Modules:
  0.0 146.9 jit_solution(3613641502709406637)
XLA Ops:
  0.6 2.4 %tracer_edges.1 = (f32[8,2,8,88]{3,2,1,0:T(8,128)}, f32[8,2,8,88]{3,2,1,0:T(8,128)}) custom-call(f32[8,2,88,1440]{3,2,1,0:T(8,128)} %refs_0_.5, f32[8,2,88,1440]{3,2,1,0:T(8,128)} %refs_0_.5), custom_call_target="tpu_custom_call" | custom-call | tf_op jit(solution)/shard_map/tracer_edges/pallas_call | solution.py:393
  3.1 2.4 %collective-permute-start.4 = (f32[8,2,8,88]{3,2,1,0:T(8,128)}, f32[8,2,8,88]{3,2,1,0:T(8,128)S(1)}, u32[]{:S(2)}, u32[]{:S(2)}) collective-permute-start(f32[8,2,8,88]{3,2,1,0:T(8,128)} %get-tuple-element.20), channel_id=1, source_target_pairs={{0,3},{1,0},{2,1},{3,2},{4,7},{5,4},{6,5},{7,6},{8,11},{9,8},{10,9... | collective-permute-start | bytes 135176 | tf_op jit(solution)/shard_map/ppermute | solution.py:37
  5.4 0.0 collective-permute-start.5
  5.4 1.0 slice_bitcast_fusion.2
  6.4 1.1 slice_bitcast_fusion
  7.5 0.0 copy-start.9
  7.5 3.4 %collective-permute-start = (f32[3,2,3,1440]{3,2,1,0:T(4,128)S(1)}, f32[3,2,3,1440]{3,2,1,0:T(4,128)S(1)}, u32[]{:S(2)}, u32[]{:S(2)}) collective-permute-start(f32[3,2,3,1440]{3,2,1,0:T(4,128)S(1)} %pad_maximum_fusion), channel_id=1, source_target_pairs={{0,4},{4,8},{8,12},{12,16},{16,20},{20,24},{24,28},{1,5},{5,9},{9,... | collective-permute-start | bytes 311048 | tf_op jit(solution)/shard_map/ppermute | solution.py:37
  11.0 1.3 collective-permute-start.1
  12.3 1.5 %fusion.8 = (f32[8,2,3,1440]{3,2,1,0:T(4,128)S(1)}, f32[8,2,3,1440]{3,2,1,0:T(4,128)S(1)}) fusion(f32[8,2,88,1440]{3,2,1,0:T(8,128)} %refs_0_.5), kind=kLoop, calls=%fused_computation.30 | loop fusion | bytes 1105920 | tf_op jit(solution)/shard_map/slice | solution.py:384
  13.8 1.3 collective-permute-start.7
  15.2 0.1 multiply_multiply_fusion
  15.3 0.1 fusion.2
  15.3 0.1 select_reduce_fusion
  15.5 0.1 fusion.3
  15.6 0.1 multiply_select_fusion
  15.6 0.0 collective-permute-done.refs_6_.refs_7_.south_ref
  15.6 0.0 copy-start.3
  15.6 3.4 %collective-permute-done.1.refs_8_.refs_9_.north_ref = f32[3,2,3,1440]{3,2,1,0:T(4,128)S(1)} collective-permute-done((f32[3,2,3,1440]{3,2,1,0:T(4,128)S(1)}, f32[3,2,3,1440]{3,2,1,0:T(4,128)S(1)}, u32[]{:S(2)}, u32[]{:S(2)}) %collective-permute-start.1) | collective-permute-done | bytes 103712 | tf_op jit(solution)/shard_map/ppermute | solution.py:37
  19.1 0.7 copy-done.4
  19.8 2.0 %field_edges.1 = (f32[3,2,8,96]{3,2,1,0:T(8,128)}, f32[3,2,8,96]{3,2,1,0:T(8,128)}) custom-call(f32[2,88,1440]{2,1,0:T(8,128)} %refs_5_.3, f32[2,88,1440]{2,1,0:T(8,128)} %refs_5_.3, f32[2,88,1440]{2,1,0:T(8,128)} %u_ref.1, f32[2,88,1440]{2,1,0:T(8,128)} %u_ref.1, f32[2,88,1440]{2,1,0:T(8,128)} %v_ref.1, f32[2,88,1440]{2,1,0:T(8,128)} %v_ref.1, ...), custom_call_target="tpu_custom_call" | custom-call | tf_op jit(solution)/shard_map/field_edges/pallas_call | solution.py:410
  21.8 1.0 collective-permute-start.2
  22.7 0.0 collective-permute-start.3
  22.7 0.1 fusion.7
  22.8 0.1 copy.15
  23.0 0.6 pad.9.waves_ref
  23.6 0.6 pad.8.rows_ref.refs_10_
  24.2 0.3 collective-permute-done.2.east_ref
  24.5 4.3 %collective-permute-start.6 = (f32[8,2,3,1440]{3,2,1,0:T(4,128)S(1)}, f32[8,2,3,1440]{3,2,1,0:T(4,128)S(1)}, u32[]{:S(2)}, u32[]{:S(2)}) collective-permute-start(f32[8,2,3,1440]{3,2,1,0:T(4,128)S(1)} %get-tuple-element.27), channel_id=1, source_target_pairs={{0,4},{4,8},{8,12},{12,16},{16,20},{20,24},{24,28},{1,5},{5,9},{9,... | collective-permute-start | bytes 829448 | tf_op jit(solution)/shard_map/ppermute | solution.py:37
  28.8 0.0 collective-permute-done.3.west_ref
  28.9 0.6 copy-done.11
  29.4 71.1 %substeps.1 = (f32[2,88,1440]{2,1,0:T(8,128)}, f32[2,88,1440]{2,1,0:T(8,128)}, f32[2,88,1440]{2,1,0:T(8,128)}, f32[2,96,1536]{2,1,0:T(8,128)}, f32[2,96,1536]{2,...) custom-call(f32[2,88,1440]{2,1,0:T(8,128)} %refs_5_.3, f32[2,88,1440]{2,1,0:T(8,128)} %u_ref.1, ...), custom_call_target="tpu_custom_call" | custom-call | flops 30000001024 | bytes 100000000 | tf_op jit(solution)/shard_map/substeps/pallas_call | solution.py:469
  100.5 0.0 collective-permute-done.4.refs_1_
  100.5 0.0 copy-start.7
  100.5 0.0 collective-permute-done.5.refs_2_
  100.6 0.0 collective-permute-done.7.refs_4_
  100.6 0.0 copy-start.5
  100.6 0.0 collective-permute-done.6.refs_3_
  100.6 0.0 copy-start.6
  100.6 0.6 copy-done.7
  101.2 0.0 copy-done.8
  101.2 0.1 copy-done.5
  101.3 0.1 copy-done.6
  101.4 41.2 %tracers.1 = f32[8,2,88,1440]{3,2,1,0:T(8,128)} custom-call(f32[8,2,88,1440]{3,2,1,0:T(8,128)} %refs_0_.5, f32[8,2,8,88]{3,2,1,0:T(8,128)} %copy-done.7, f32[8,2,8,88]{3,2,1,0:T(8,128)} %copy-done.8, f32[8,2,3,1440]{3,2,1,0:T(4,128)} %copy-done.6, f32[8,2,3,1440]{3,2,1,0:T(4,128)} %copy-done.5, f32[2,88,1440]{2,1,0:T(8,128)} %refs_5_.3, ...), custom_call_target="tpu_custom_call" | custom-call | tf_op jit(solution)/shard_map/tracers/pallas_call | solution.py:500
  142.6 1.0 copy.19
  143.6 0.6 copy-done.1
  144.3 1.0 copy.20
  145.2 0.6 copy-done
  145.9 1.0 copy.21
  (19 shorter events, 0.2 us)
Async XLA Ops:
  3.1 97.5 %collective-permute-start.4 = (f32[8,2,8,88]{3,2,1,0:T(8,128)}, f32[8,2,8,88]{3,2,1,0:T(8,128)S(1)}, u32[]{:S(2)}, u32[]{:S(2)}) collective-permute-start(f32[8,2,8,88]{3,2,1,0:T(8,128)} %get-tuple-element.20), channel_id=1, source_target_pairs={{0,3},{1,0},{2,1},{3,2},{4,7},{5,4},{6,5},{7,6},{8,11},{9,8},{10,9... | collective-permute-start | bytes 135176 | tf_op jit(solution)/shard_map/ppermute | solution.py:37
  5.4 95.1 %collective-permute-start.5 = (f32[8,2,8,88]{3,2,1,0:T(8,128)}, f32[8,2,8,88]{3,2,1,0:T(8,128)S(1)}, u32[]{:S(2)}, u32[]{:S(2)}) collective-permute-start(f32[8,2,8,88]{3,2,1,0:T(8,128)} %get-tuple-element.21), channel_id=1, source_target_pairs={{0,1},{1,2},{2,3},{3,0},{4,5},{5,6},{6,7},{7,4},{8,9},{9,10},{10,1... | collective-permute-start | bytes 135176 | tf_op jit(solution)/shard_map/ppermute | solution.py:37
  7.5 7.9 %copy-start.9 = (s32[176]{0:T(256)S(1)}, s32[176]{0:T(256)}, u32[]{:S(2)}) copy-start(s32[176]{0:T(256)} %param.13) | copy-start | bytes 2116
  7.5 8.1 %collective-permute-start = (f32[3,2,3,1440]{3,2,1,0:T(4,128)S(1)}, f32[3,2,3,1440]{3,2,1,0:T(4,128)S(1)}, u32[]{:S(2)}, u32[]{:S(2)}) collective-permute-start(f32[3,2,3,1440]{3,2,1,0:T(4,128)S(1)} %pad_maximum_fusion), channel_id=1, source_target_pairs={{0,4},{4,8},{8,12},{12,16},{16,20},{20,24},{24,28},{1,5},{5,9},{9,... | collective-permute-start | bytes 311048 | tf_op jit(solution)/shard_map/ppermute | solution.py:37
  11.0 8.1 %collective-permute-start.1 = (f32[3,2,3,1440]{3,2,1,0:T(4,128)S(1)}, f32[3,2,3,1440]{3,2,1,0:T(4,128)S(1)}, u32[]{:S(2)}, u32[]{:S(2)}) collective-permute-start(f32[3,2,3,1440]{3,2,1,0:T(4,128)S(1)} %pad_maximum_fusion.1), channel_id=1, source_target_pairs={{4,0},{8,4},{12,8},{16,12},{20,16},{24,20},{28,24},{5,1},{9,5},{13... | collective-permute-start | bytes 311048 | tf_op jit(solution)/shard_map/ppermute | solution.py:37
  13.8 86.7 %collective-permute-start.7 = (f32[8,2,3,1440]{3,2,1,0:T(4,128)S(1)}, f32[8,2,3,1440]{3,2,1,0:T(4,128)S(1)}, u32[]{:S(2)}, u32[]{:S(2)}) collective-permute-start(f32[8,2,3,1440]{3,2,1,0:T(4,128)S(1)} %get-tuple-element.26), channel_id=1, source_target_pairs={{4,0},{8,4},{12,8},{16,12},{20,16},{24,20},{28,24},{5,1},{9,5},{13... | collective-permute-start | bytes 829448 | tf_op jit(solution)/shard_map/ppermute | solution.py:37
  15.6 3.5 %copy-start.3 = (f32[3,2,3,1440]{3,2,1,0:T(4,128)}, f32[3,2,3,1440]{3,2,1,0:T(4,128)S(1)}, u32[]{:S(2)}) copy-start(f32[3,2,3,1440]{3,2,1,0:T(4,128)S(1)} %collective-permute-done.refs_6_.refs_7_.south_ref) | copy-start | bytes 311044
  19.1 0.7 copy-start.4
  21.8 2.7 %collective-permute-start.2 = (f32[3,2,8,96]{3,2,1,0:T(8,128)}, f32[3,2,8,96]{3,2,1,0:T(8,128)S(1)}, u32[]{:S(2)}, u32[]{:S(2)}) collective-permute-start(f32[3,2,8,96]{3,2,1,0:T(8,128)} %get-tuple-element.15), channel_id=1, source_target_pairs={{0,3},{1,0},{2,1},{3,2},{4,7},{5,4},{6,5},{7,6},{8,11},{9,8},{10,9... | collective-permute-start | bytes 55304 | tf_op jit(solution)/shard_map/ppermute | solution.py:37
  22.7 6.1 %collective-permute-start.3 = (f32[3,2,8,96]{3,2,1,0:T(8,128)}, f32[3,2,8,96]{3,2,1,0:T(8,128)S(1)}, u32[]{:S(2)}, u32[]{:S(2)}) collective-permute-start(f32[3,2,8,96]{3,2,1,0:T(8,128)} %get-tuple-element.16), channel_id=1, source_target_pairs={{0,1},{1,2},{2,3},{3,0},{4,5},{5,6},{6,7},{7,4},{8,9},{9,10},{10,1... | collective-permute-start | bytes 55304 | tf_op jit(solution)/shard_map/ppermute | solution.py:37
  24.5 4.4 %copy-start.10 = (f32[3,2,8,96]{3,2,1,0:T(8,128)}, f32[3,2,8,96]{3,2,1,0:T(8,128)S(1)}, u32[]{:S(2)}) copy-start(f32[3,2,8,96]{3,2,1,0:T(8,128)S(1)} %collective-permute-done.2.east_ref) | copy-start | bytes 55300
  24.5 76.1 %collective-permute-start.6 = (f32[8,2,3,1440]{3,2,1,0:T(4,128)S(1)}, f32[8,2,3,1440]{3,2,1,0:T(4,128)S(1)}, u32[]{:S(2)}, u32[]{:S(2)}) collective-permute-start(f32[8,2,3,1440]{3,2,1,0:T(4,128)S(1)} %get-tuple-element.27), channel_id=1, source_target_pairs={{0,4},{4,8},{8,12},{12,16},{16,20},{20,24},{24,28},{1,5},{5,9},{9,... | collective-permute-start | bytes 829448 | tf_op jit(solution)/shard_map/ppermute | solution.py:37
  28.8 0.6 copy-start.11
  100.5 0.6 copy-start.7
  100.5 0.6 copy-start.8
  100.6 0.7 copy-start.5
  100.6 0.9 copy-start.6
  101.4 41.2 %copy-start.2 = (f32[2,88,1440]{2,1,0:T(8,128)S(1)}, f32[2,88,1440]{2,1,0:T(8,128)}, u32[]{:S(2)}) copy-start(f32[2,88,1440]{2,1,0:T(8,128)} %get-tuple-element.48) | copy-start | bytes 3041284
  142.6 1.6 %copy-start.1 = (f32[2,88,1440]{2,1,0:T(8,128)S(1)}, f32[2,88,1440]{2,1,0:T(8,128)}, u32[]{:S(2)}) copy-start(f32[2,88,1440]{2,1,0:T(8,128)} %get-tuple-element.49) | copy-start | bytes 3041284
  144.3 1.6 %copy-start = (f32[2,88,1440]{2,1,0:T(8,128)S(1)}, f32[2,88,1440]{2,1,0:T(8,128)}, u32[]{:S(2)}) copy-start(f32[2,88,1440]{2,1,0:T(8,128)} %get-tuple-element.50) | copy-start | bytes 3041284
